TPU v7x, 128 devices: a whole 4x4x4 slice. The times are simulated.
128 devices in a mesh: pipe: 16 (over z_hi, x, core), tensor: 8 (over y, z_lo).
Axes of the slice: x: 4, y: 4, z: 4 (z_hi: 2, z_lo: 2; z = z_hi * 2 + z_lo), core: 2. Of those that a mesh axis runs over, the one named last changes fastest.
Arguments:
- entry_symbol_ids: int32 [1024], replicated, may hold values from 0 to 131071
- lookup_table_matrix: bfloat16 [131072, 4096], P('pipe', 'tensor'), may hold values from -6 to 6
- pending_batches: bfloat16 [16384, 4096], P(('pipe', 'tensor')), may hold values from -6 to 6
- scale_factors: float32 [16, 4096], P('pipe'), may hold values from 0.25 to 1.75
- query_projector: bfloat16 [16, 4096, 4096], P('pipe', None, 'tensor'), may hold values from -0.0625 to 0.0625
- key_projector: bfloat16 [16, 4096, 512], P('pipe', None, 'tensor'), may hold values from -1.25 to 1.25
- value_projector: bfloat16 [16, 4096, 512], P('pipe', None, 'tensor'), may hold values from -0.09375 to 0.09375
- result_projector: bfloat16 [16, 4096, 4096], P('pipe', 'tensor'), may hold values from -0.75 to 0.75
Outputs:
- block_results: float32 [16384, 4096], P(('pipe', 'tensor'))
- second_out: float32 [16384, 4096], P(('pipe', 'tensor'))
All inputs are finite; a program needn't handle non-finite values.
Results may differ from a plain program's by a relative error of at most 0.035.
The roundings to bfloat16 on the way count: a program that leaves them out, or rounds other values in their place, can miss the bound.
Values may be sent and summed in bfloat16 or wider, within the bound.
A program may use at most 192 MiB of HBM per device.

v0:
```python
import math

import jax
import jax.numpy as jnp
from jax import lax
from jax.sharding import PartitionSpec as P

HEAD_DIM = 128


def from_partner(block, axis, distance):
    count = lax.axis_size(axis)
    route = []
    for low in range(count):
        high = low | 1 << distance
        if high != low and high < count:
            route += [(low, high), (high, low)]
    return lax.ppermute(block, axis, route)


def passed_along(block, axis, distance):
    devices = range(lax.axis_size(axis))
    route = [(i - distance, i) for i in devices if i - distance in devices]
    return lax.ppermute(block, axis, route)


def softmax_block(query_block, key_head, value_head, first_row):
    block_len = query_block.shape[1]
    seq_len = key_head.shape[0]
    scores = jnp.einsum(
        "hqd,kd->hqk", query_block, key_head, preferred_element_type=jnp.float32
    ) * HEAD_DIM ** (-0.5)
    query_pos = first_row + jnp.arange(block_len, dtype=jnp.int32)
    key_pos = jnp.arange(seq_len, dtype=jnp.int32)
    causal_mask = query_pos[:, None] >= key_pos[None, :]
    scores = jnp.where(causal_mask[None], scores, jnp.float32(-1e30))
    top_score = jnp.max(scores, axis=2, keepdims=True)
    exp_scores = jnp.exp(scores - top_score)
    attn_weights = (exp_scores / jnp.sum(exp_scores, axis=2, keepdims=True)).astype(jnp.bfloat16)
    return jnp.einsum(
        "hqk,kd->hqd", attn_weights, value_head, preferred_element_type=jnp.float32
    ).astype(jnp.bfloat16)


def body(
    entry_symbol_ids,
    lookup_table_matrix,
    pending_batches,
    scale_factors,
    query_projector,
    key_projector,
    value_projector,
    result_projector,
):
    tensor_count = lax.axis_size("tensor")
    pipe_pos = lax.axis_index("pipe")
    tensor_pos = lax.axis_index("tensor")
    number_lines = pending_batches.shape[0]
    feature_extent = pending_batches.shape[1]
    query_cols = query_projector.shape[2]
    kv_cols = key_projector.shape[2]
    spread = HEAD_DIM // kv_cols
    gain_full = scale_factors[0]
    out_mat = result_projector[0]
    vocab_dev = lookup_table_matrix.shape[0]
    local_index = entry_symbol_ids - pipe_pos * vocab_dev
    inside = (local_index >= 0) & (local_index < vocab_dev)
    looked = jnp.take(lookup_table_matrix, jnp.clip(local_index, 0, vocab_dev - 1), axis=0)
    looked = jnp.where(inside[:, None], looked, jnp.zeros_like(looked))
    exchanged = lax.all_to_all(
        looked.reshape(tensor_count, number_lines, -1),
        "tensor",
        split_axis=0,
        concat_axis=2,
        tiled=True,
    )
    laid_out = exchanged.reshape(number_lines, feature_extent)
    entering = lax.psum(laid_out.astype(jnp.float32).astype(jnp.bfloat16), "pipe")
    project_mat = jnp.concatenate(
        [query_projector[0], key_projector[0], value_projector[0]], axis=1
    )

    def project(shard_piece):
        return jnp.dot(shard_piece, project_mat, preferred_element_type=jnp.float32).astype(
            jnp.bfloat16
        )

    def shared_key_mixer(x_rows):
        x_float = x_rows.astype(jnp.float32)
        normed = (
            x_float
            * lax.rsqrt(jnp.mean(x_float * x_float, axis=1, keepdims=True) + 1e-05)
            * gain_full
        ).astype(jnp.bfloat16)
        projected = project(lax.all_gather(normed, "tensor", axis=0, tiled=True))
        seq_len = projected.shape[0]
        queries = projected[:, :query_cols]
        packed_rows = projected[:, query_cols:]
        partner_rows = from_partner(packed_rows, "tensor", 0)
        is_high = tensor_pos // (1 << 0) % 2 == 1
        packed_rows = jnp.where(
            is_high,
            jnp.concatenate([partner_rows, packed_rows], axis=1),
            jnp.concatenate([packed_rows, partner_rows], axis=1),
        )
        split_rows = packed_rows.reshape(seq_len, spread, 2, kv_cols)
        key_head = split_rows[:, :, 0, :].reshape(seq_len, HEAD_DIM)
        value_head = split_rows[:, :, 1, :].reshape(seq_len, HEAD_DIM)
        heads_dev = query_cols // HEAD_DIM
        block_len = math.gcd(seq_len, 512)
        block_count = seq_len // block_len
        query_blocks = queries.reshape(block_count, block_len, heads_dev, HEAD_DIM).transpose(
            0, 2, 1, 3
        )
        first_rows = jnp.arange(block_count, dtype=jnp.int32) * block_len

        def one_block(operands):
            return softmax_block(operands[0], key_head, value_head, operands[1])

        context = lax.map(one_block, (query_blocks, first_rows))
        context = context.transpose(0, 2, 1, 3).reshape(seq_len, query_cols)
        summed = lax.psum_scatter(
            jnp.dot(context, out_mat, preferred_element_type=jnp.float32),
            "tensor",
            scatter_dimension=0,
            tiled=True,
        )
        return x_float + summed

    block_results = shared_key_mixer(pending_batches)
    arrived = passed_along(block_results, "pipe", 1)
    second_in = jnp.where(pipe_pos == 0, entering.astype(jnp.float32), arrived)
    second_out = shared_key_mixer(second_in)
    return (block_results, second_out)


def solution(mesh):
    in_specs = (
        P(),
        P("pipe", "tensor"),
        P(("pipe", "tensor"), None),
        P("pipe", None),
        P("pipe", None, "tensor"),
        P("pipe", None, "tensor"),
        P("pipe", None, "tensor"),
        P("pipe", "tensor", None),
    )
    out_specs = (P(("pipe", "tensor"), None), P(("pipe", "tensor"), None))
    return jax.shard_map(body, mesh=mesh, in_specs=in_specs, out_specs=out_specs, check_vma=False)
```

profile of v0, /device:TPU:1, one launch (start us, length us, event | category | flops | bytes accessed | tf_op | source)
XLA Modules:
  0.0 1335.3 jit_solution(14354629824966740216)
XLA Ops:
  9.6 2.5 fusion.72
  14.3 169.7 %all-gather.3.cloned.1.call-done = bf16[1024,4096]{1,0:T(8,128)(2,1)} async-done(((bf16[128,4096]{1,0:T(8,128)(2,1)}), bf16[1024,4096]{1,0:T(8,128)(2,1)}) %all-gather.3.cloned.1.call-update) | async-done | bytes 8388624 | tf_op jit(solution)/shard_map/all_gather | solution.py:95
  183.9 10.2 fusion.75
  196.7 5.6 collective-permute-done
  203.9 23.8 %while.20 = (s32[]{:T(128)}, bf16[2,4,512,128]{3,2,1,0:T(8,128)(2,1)S(1)}, s32[2]{0:T(128)S(1)}, bf16[2,4,512,128]{3,2,1,0:T(8,128)(2,1)S(1)}, bf16[1024,128]{1,...) while((s32[]{:T(128)}, bf16[2,4,512,128]{3,2,1,0:T(8,128)(2,1)S(1)}, s32[2]{0:T(128)S(1)}, ...), condition=%wide.region_4.5_spmd, body=%wide.region_1.4_spmd.sunk | while | flops 1087112704 | bytes 19419244 | solution.py:120
  205.6 5.4 fusion.120
  210.9 4.9 fusion.121
  217.4 5.4 fusion.120
  222.8 4.9 fusion.121
  228.5 10.3 fusion.68
  239.5 8.4 gather_fusion
  248.0 324.0 %reduce-scatter.3.cloned.1.call-done = f32[128,4096]{1,0:T(8,128)} async-done(((f32[1024,4096]{1,0:T(8,128)}), f32[128,4096]{1,0:T(8,128)}) %reduce-scatter.3.cloned.1.call-update) | async-done | bytes 2097168 | tf_op jit(solution)/shard_map/reduce_scatter | solution.py:122
  572.0 3.1 convert_add_fusion
  575.1 3.6 collective-permute-start.1
  579.2 38.0 %all_to_all.15 = bf16[8,128,512]{2,1,0:T(8,128)(2,1)S(1)} all-to-all(bf16[8,128,512]{2,1,0:T(8,128)(2,1)S(1)} %select_select_fusion), channel_id=1, replica_groups=mesh['pipe'=16,'tensor'=8] {'tensor'}, dimensions={0} | all-to-all | bytes 2097152 | tf_op jit(solution)/shard_map/all_to_all | solution.py:70
  618.4 137.3 %all-reduce.2.cloned.1.call-done = bf16[128,4096]{1,0:T(8,128)(2,1)} async-done(((bf16[128,4096]{1,0:T(8,128)(2,1)}), bf16[128,4096]{1,0:T(8,128)(2,1)}) %all-reduce.2.cloned.1.call-update) | async-done | bytes 1048592 | tf_op jit(solution)/shard_map/psum | solution.py:78
  755.7 1.6 multiply_reduce_fusion
  757.3 2.5 multiply_convert_fusion
  760.2 169.4 %all-gather.5.cloned.1.call-done = bf16[1024,4096]{1,0:T(8,128)(2,1)} async-done(((bf16[128,4096]{1,0:T(8,128)(2,1)}), bf16[1024,4096]{1,0:T(8,128)(2,1)}) %all-gather.5.cloned.1.call-update) | async-done | bytes 8388624 | tf_op jit(solution)/shard_map/all_gather | solution.py:95
  929.5 10.6 fusion.76
  940.6 1.6 reshape.117
  942.1 3.7 copy.51
  945.8 1.9 collective-permute-done.2
  950.4 29.0 %while.21 = (s32[]{:T(128)}, bf16[2,4,512,128]{3,2,1,0:T(8,128)(2,1)}, s32[2]{0:T(128)S(1)}, bf16[2,4,512,128]{3,2,1,0:T(8,128)(2,1)}, bf16[1024,128]{1,0:T(8,12...) while((s32[]{:T(128)}, bf16[2,4,512,128]{3,2,1,0:T(8,128)(2,1)}, s32[2]{0:T(128)S(1)}, ...), condition=%wide.region_11.12_spmd, body=%wide.region_8.11_spmd.sunk | while | flops 1087112704 | bytes 19419244 | solution.py:120
  952.1 7.3 fusion.125
  959.4 5.5 fusion.126
  966.6 7.3 fusion.125
  973.9 5.5 fusion.126
  979.4 2.0 copy.58
  981.4 10.3 fusion.66
  991.8 333.1 %reduce-scatter.5.cloned.1.call-done = f32[128,4096]{1,0:T(8,128)} async-done(((f32[1024,4096]{1,0:T(8,128)}), f32[128,4096]{1,0:T(8,128)}) %reduce-scatter.5.cloned.1.call-update) | async-done | bytes 2097168 | tf_op jit(solution)/shard_map/reduce_scatter | solution.py:122
  1324.9 3.2 fusion.81
  (68 shorter events, 20.9 us)
Async XLA Ops:
  8.0 5.8 copy-start.5
  8.0 175.9 %all-gather.3.cloned.1.call-start = ((), (), s32[]{:S(2)}) async-start(), calls=%async_computation.3 | async-start | bytes 9437184 | tf_op jit(solution)/shard_map/all_gather | solution.py:95
  12.2 559.8 %reduce-scatter.3.cloned.1.call-start = ((), (), s32[]{:S(2)}) async-start(), calls=%async_computation.4 | async-start | bytes 18874368 | tf_op jit(solution)/shard_map/reduce_scatter | solution.py:122
  13.8 180.4 %copy-start.2 = (bf16[4096,64]{1,0:T(8,128)(2,1)}, bf16[4096,64]{1,0:T(8,128)(2,1)S(1)}, u32[]{:S(2)}) copy-start(bf16[4096,64]{1,0:T(8,128)(2,1)S(1)} %copy.40) | copy-start | bytes 1572868
  14.3 179.9 %copy-start.4 = (bf16[4096,64]{1,0:T(8,128)(2,1)}, bf16[4096,64]{1,0:T(8,128)(2,1)S(1)}, u32[]{:S(2)}) copy-start(bf16[4096,64]{1,0:T(8,128)(2,1)S(1)} %copy.41) | copy-start | bytes 1572868
  194.9 7.4 collective-permute-start
  238.8 0.7 copy-start.7
  238.9 333.1 %copy-start = (bf16[128,4096]{1,0:T(8,128)(2,1)S(1)}, bf16[128,4096]{1,0:T(8,128)(2,1)}, u32[]{:S(2)}) copy-start(bf16[128,4096]{1,0:T(8,128)(2,1)} %param.14) | copy-start | bytes 3145732
  238.9 516.9 %all-reduce.2.cloned.1.call-start = ((), (), s32[]{:S(2)}) async-start(), calls=%async_computation.5 | async-start | bytes 2097152 | tf_op jit(solution)/shard_map/psum | solution.py:78
  575.1 180.6 %collective-permute-start.1 = (f32[128,4096]{1,0:T(8,128)}, f32[128,4096]{1,0:T(8,128)S(1)}, u32[]{:S(2)}, u32[]{:S(2)}) collective-permute-start(f32[128,4096]{1,0:T(8,128)} %convert_add_fusion), channel_id=1, source_target_pairs={{0,8},{8,16},{16,24},{24,32},{32,40},{40,48},{48,56},{56,64},{64,7... | collective-permute-start | bytes 6291464 | tf_op jit(solution)/shard_map/ppermute | solution.py:24
  578.7 178.6 %copy-start.6 = (f32[1,4096]{1,0:T(1,128)S(1)}, f32[1,4096]{1,0:T(1,128)}, u32[]{:S(2)}) copy-start(f32[1,4096]{1,0:T(1,128)} %param.15) | copy-start | bytes 49156
  618.3 311.2 %copy-start.3 = (bf16[4096,64]{1,0:T(8,128)(2,1)S(1)}, bf16[4096,64]{1,0:T(8,128)(2,1)}, u32[]{:S(2)}) copy-start(bf16[4096,64]{1,0:T(8,128)(2,1)} %copy-done.2) | copy-start | bytes 1572868
  618.4 311.2 %all-gather.5.cloned.1.call-start = ((), (), s32[]{:S(2)}) async-start(), calls=%async_computation.6 | async-start | bytes 9437184 | tf_op jit(solution)/shard_map/all_gather | solution.py:95
  759.9 565.0 %reduce-scatter.5.cloned.1.call-start = ((), (), s32[]{:S(2)}) async-start(), calls=%async_computation.7 | async-start | bytes 18874368 | tf_op jit(solution)/shard_map/reduce_scatter | solution.py:122
  940.1 7.6 collective-permute-start.2
  991.7 333.2 %copy-start.1 = (bf16[128,4096]{1,0:T(8,128)(2,1)S(1)}, bf16[128,4096]{1,0:T(8,128)(2,1)}, u32[]{:S(2)}) copy-start(bf16[128,4096]{1,0:T(8,128)(2,1)} %all-reduce.2.cloned.1.call-done) | copy-start | bytes 3145732
Sparse Core Ops, SparseCore 0:
  12.3 171.5 all-gather.2
  239.0 332.9 reduce-scatter.2
  760.0 169.4 all-gather.4
  991.9 332.9 reduce-scatter.4
Sparse Core Ops, SparseCore 1:
  618.4 137.2 all-reduce.1
where the time goes:
time: 1340 us
  waiting for transfers between devices  1140 us (85%)
  matrix products  87.5 us (7%)
  blocking collectives  38 us (3%)
  local copies, waits for them, and re-layouts  27.4 us (2%)
  other arithmetic  21.4 us (2%)
  between operations  15.5 us (1%)
    reduce_scatter x2, waiting for transfers between devices, shared_key_mixer(): lax.psum_scatter(jnp.dot(context, out_mat, preferred_element_type=jnp.flo...  657 us
    all_gather x2, waiting for transfers between devices, shared_key_mixer(): projected = project(lax.all_gather(normed, 'tensor', axis=0, tiled=True))  339 us
    psum x1, waiting for transfers between devices, body(): lax.psum(laid_out.astype(jnp.float32).astype(jnp.bfloat16), 'pipe')  137 us
    all_to_all x1, blocking collectives, body(): lax.all_to_all(looked.reshape(tensor_count, number_lines, -1), 'tensor',...  38 us
  transfers between devices with their start and end apart: 8, of which 7 were waited for; matrix products, arithmetic and copies ran while one was open for 1% of the time, Pallas kernels for 0%

commit v1 on v0

v1 whole, which is shorter than its diff:
```python
import functools

import jax
import jax.numpy as jnp
from jax import lax
from jax.experimental import pallas as pl
from jax.experimental.pallas import tpu as pltpu
from jax.sharding import PartitionSpec as P

HEAD_DIM = 128
MESH = pl.DeviceIdType.MESH
BOTH = ("pipe", "tensor")
RING = 4
TOKENS = 1024
ROWS = 128
WIDTH = 4096
HEADS_DEV = 4
PAIR = 2 * ROWS
HALF = ROWS // 2


def flat(pipe, tensor):
    return pipe * 8 + tensor


def physical(section, block):
    return flat(2 * (section // 2) + block % 2, 2 * (block // 2) + section % 2)


def traded(array):
    route = [(flat(s, t), physical(s, t)) for s in range(16) for t in range(8)]
    return lax.ppermute(array, BOTH, route)


def to_next_section(array):
    route = [(physical(s, t), physical(s + 1, t)) for s in range(15) for t in range(8)]
    return lax.ppermute(array, BOTH, route)


def layer_kernel(
    x_ref, gain_ref, wq_hbm, kv_hbm, wo_hbm, out_ref,
    w_in, w_out, normed, q_s, k_s, v_s, ctx, own_part, sib_out, sib_in, ring_out, relay, arrived,
    load_sem, kv_sem, ag_send, ag_recv, sib_send, sib_recv, ring_send, ring_recv,
):
    pipe = lax.axis_index("pipe")
    tensor = lax.axis_index("tensor")
    core = lax.rem(pipe, 2)
    y = lax.div(tensor, 2)
    z_lo = lax.rem(tensor, 2)
    y_up = lax.rem(y + 1, RING)
    y_far = lax.rem(y + 2, RING)
    y_down = lax.rem(y + 3, RING)
    sibling = (pipe + 1 - 2 * core, tensor)
    up = (pipe, 2 * y_up + z_lo)
    down = (pipe, 2 * y_down + z_lo)

    barrier = pltpu.get_barrier_semaphore()
    for other in (sibling, up, down):
        pl.semaphore_signal(barrier, inc=1, device_id=other, device_id_type=MESH)

    load_q = pltpu.make_async_copy(wq_hbm, w_in.at[:, pl.ds(0, 512)], load_sem.at[0])
    kv_cols = pl.ds(pl.multiple_of(512 + core * 128, 128), 128)
    load_kv = pltpu.make_async_copy(kv_hbm, w_in.at[:, kv_cols], load_sem.at[1])
    load_o = pltpu.make_async_copy(wo_hbm, w_out, load_sem.at[2])
    load_q.start()
    load_kv.start()
    load_o.start()

    def norm_rows(step, carry):
        rows = pl.ds(pl.multiple_of(step * 16, 16), 16)
        x = x_ref[rows, :].astype(jnp.float32)
        scale = lax.rsqrt(jnp.mean(x * x, axis=1, keepdims=True) + 1e-05)
        into = pl.ds(pl.multiple_of(core * ROWS + step * 16, 16), 16)
        normed[y, into, :] = (x * scale * gain_ref[...]).astype(jnp.bfloat16)
        return carry

    lax.fori_loop(0, ROWS // 16, norm_rows, 0)
    pl.semaphore_wait(barrier, 3)

    sends = []

    def send(src, dst, send_sem, recv_sem, device):
        copy = pltpu.make_async_remote_copy(
            src_ref=src, dst_ref=dst, send_sem=send_sem, recv_sem=recv_sem,
            device_id=device, device_id_type=MESH,
        )
        copy.start()
        sends.append(copy)

    def piece(chip, side, half):
        return normed.at[chip, pl.ds(pl.multiple_of(side * ROWS + half * HALF, HALF), HALF), :]

    def gather(chip, side, half, device):
        part = piece(chip, side, half)
        send(part, part, ag_send.at[len(sends)], ag_recv.at[chip, side, half], device)

    def wait_piece(chip, side, half):
        part = piece(chip, side, half)
        pltpu.make_async_remote_copy(
            src_ref=part, dst_ref=part, send_sem=ag_send.at[0], recv_sem=ag_recv.at[chip, side, half],
            device_id=sibling, device_id_type=MESH,
        ).wait_recv()

    other = 1 - core
    gather(y, core, 0, up)
    gather(y, core, 1, down)
    gather(y, core, 0, sibling)
    gather(y, core, 1, sibling)
    gather(y, core, 1, up)
    gather(y, core, 0, down)
    kv_view = w_in.at[:, kv_cols]
    load_kv.wait()
    send(kv_view, kv_view, kv_sem.at[0], kv_sem.at[1], sibling)
    load_q.wait()
    kv_other = w_in.at[:, pl.ds(pl.multiple_of(512 + other * 128, 128), 128)]
    pltpu.make_async_remote_copy(
        src_ref=kv_other, dst_ref=kv_other, send_sem=kv_sem.at[0], recv_sem=kv_sem.at[1],
        device_id=sibling, device_id_type=MESH,
    ).wait_recv()

    def project(chip):
        rows = pl.ds(pl.multiple_of(chip * PAIR, PAIR), PAIR)

        def two_heads(n, carry):
            cols = pl.ds(pl.multiple_of(n * 256, 256), 256)
            res = jnp.dot(normed[chip], w_in[:, cols], preferred_element_type=jnp.float32)
            q_s[2 * n, rows, :] = res[:, :128].astype(jnp.bfloat16)
            q_s[2 * n + 1, rows, :] = res[:, 128:].astype(jnp.bfloat16)
            return carry

        lax.fori_loop(0, 2, two_heads, 0)
        res = jnp.dot(normed[chip], w_in[:, 512:768], preferred_element_type=jnp.float32)
        k_s[rows, :] = jnp.concatenate([res[:, 0:64], res[:, 128:192]], axis=1).astype(jnp.bfloat16)
        v_s[rows, :] = jnp.concatenate([res[:, 64:128], res[:, 192:256]], axis=1).astype(jnp.bfloat16)

    wait_piece(y, other, 0)
    wait_piece(y, other, 1)
    project(y)
    wait_piece(y_down, core, 0)
    gather(y_down, core, 0, up)
    gather(y_down, core, 0, sibling)
    wait_piece(y_up, core, 1)
    gather(y_up, core, 1, down)
    gather(y_up, core, 1, sibling)
    wait_piece(y_down, core, 1)
    gather(y_down, core, 1, sibling)
    wait_piece(y_up, core, 0)
    gather(y_up, core, 0, sibling)
    for chip in (y_down, y_up):
        wait_piece(chip, other, 0)
        wait_piece(chip, other, 1)
        project(chip)
    wait_piece(y_far, core, 0)
    gather(y_far, core, 0, sibling)
    wait_piece(y_far, core, 1)
    gather(y_far, core, 1, sibling)
    wait_piece(y_far, other, 0)
    wait_piece(y_far, other, 1)
    project(y_far)

    scale = HEAD_DIM ** (-0.5)

    def head(h, carry):
        cols = pl.ds(pl.multiple_of(h * HEAD_DIM, HEAD_DIM), HEAD_DIM)
        for i in range(RING):
            keys = PAIR * (i + 1)
            scores = lax.dot_general(
                q_s[h, PAIR * i : keys, :], k_s[:keys, :], (((1,), (1,)), ((), ())),
                preferred_element_type=jnp.float32,
            ) * scale
            q_pos = PAIR * i + lax.broadcasted_iota(jnp.int32, (PAIR, keys), 0)
            k_pos = lax.broadcasted_iota(jnp.int32, (PAIR, keys), 1)
            scores = jnp.where(q_pos >= k_pos, scores, -1e30)
            top = jnp.max(scores, axis=1, keepdims=True)
            exps = jnp.exp(scores - top)
            weights = (exps * (1.0 / jnp.sum(exps, axis=1, keepdims=True))).astype(jnp.bfloat16)
            mixed = jnp.dot(weights, v_s[:keys, :], preferred_element_type=jnp.float32)
            ctx[i, :, cols] = mixed.astype(jnp.bfloat16)
        return carry

    lax.fori_loop(0, HEADS_DEV, head, 0)

    load_o.wait()

    def out_project(slot, chip):
        def columns(n, carry):
            cols = pl.ds(pl.multiple_of(n * 512, 512), 512)
            res = jnp.dot(ctx[chip], w_out[:, cols], preferred_element_type=jnp.float32)
            low, high = res[:ROWS], res[ROWS:]
            own_part[slot, :, cols] = jnp.where(core == 0, low, high)
            sib_out[slot, :, cols] = jnp.where(core == 0, high, low).astype(jnp.bfloat16)
            return carry

        lax.fori_loop(0, WIDTH // 512, columns, 0)
        send(sib_out.at[slot], sib_in.at[slot], sib_send.at[slot], sib_recv.at[slot], sibling)

    def wait_recv(ref, sem):
        pltpu.make_async_remote_copy(
            src_ref=ref, dst_ref=ref, send_sem=sib_send.at[0], recv_sem=sem,
            device_id=sibling, device_id_type=MESH,
        ).wait_recv()

    def combine(slot, first, count, relayed):
        def rows_step(step, carry):
            rows = pl.ds(pl.multiple_of(first + step * 16, 16), 16)
            total = own_part[slot, rows, :] + sib_in[slot, rows, :].astype(jnp.float32)
            if relayed is not None:
                from_rows = pl.ds(pl.multiple_of(step * 16, 16), 16)
                total = total + relay[relayed, from_rows, :].astype(jnp.float32)
            ring_out[slot, rows, :] = total.astype(jnp.bfloat16)
            return carry

        lax.fori_loop(0, count // 16, rows_step, 0)

    out_project(0, y_far)
    out_project(1, y_up)
    wait_recv(sib_in.at[0], sib_recv.at[0])
    combine(0, 0, ROWS, None)
    send(ring_out.at[0, pl.ds(0, HALF)], relay.at[0], ring_send.at[0], ring_recv.at[0], up)
    send(ring_out.at[0, pl.ds(HALF, HALF)], relay.at[1], ring_send.at[1], ring_recv.at[1], down)
    out_project(2, y_down)
    wait_recv(sib_in.at[1], sib_recv.at[1])
    combine(1, HALF, HALF, None)
    send(ring_out.at[1, pl.ds(HALF, HALF)], arrived.at[0, pl.ds(HALF, HALF)], ring_send.at[2], ring_recv.at[2], up)
    wait_recv(sib_in.at[2], sib_recv.at[2])
    combine(2, 0, HALF, None)
    send(ring_out.at[2, pl.ds(0, HALF)], arrived.at[1, pl.ds(0, HALF)], ring_send.at[3], ring_recv.at[3], down)
    out_project(3, y)
    wait_recv(relay.at[0], ring_recv.at[0])
    combine(1, 0, HALF, 0)
    send(ring_out.at[1, pl.ds(0, HALF)], arrived.at[0, pl.ds(0, HALF)], ring_send.at[4], ring_recv.at[4], up)
    wait_recv(relay.at[1], ring_recv.at[1])
    combine(2, HALF, HALF, 1)
    send(ring_out.at[2, pl.ds(HALF, HALF)], arrived.at[1, pl.ds(HALF, HALF)], ring_send.at[5], ring_recv.at[5], down)
    wait_recv(sib_in.at[3], sib_recv.at[3])

    def finish(first):
        def rows_step(step, carry):
            rows = pl.ds(pl.multiple_of(first + step * 16, 16), 16)
            total = own_part[3, rows, :] + sib_in[3, rows, :].astype(jnp.float32)
            total = total + arrived[0, rows, :].astype(jnp.float32)
            total = total + arrived[1, rows, :].astype(jnp.float32)
            out_ref[rows, :] = x_ref[rows, :].astype(jnp.float32) + total
            return carry

        lax.fori_loop(0, HALF // 16, rows_step, 0)

    for sem in (2, 3, 4, 5):
        slot = 0 if sem in (2, 4) else 1
        first = HALF if sem in (2, 5) else 0
        wait_recv(arrived.at[slot, pl.ds(first, HALF)], ring_recv.at[sem])
    finish(0)
    finish(HALF)
    for copy in sends:
        copy.wait_send()


def layer(x, gain, wq, kv, wo):
    bf16, f32 = jnp.bfloat16, jnp.float32
    dma = pltpu.SemaphoreType.DMA
    vmem = pl.BlockSpec(memory_space=pltpu.VMEM)
    hbm = pl.BlockSpec(memory_space=pl.ANY)
    return pl.pallas_call(
        layer_kernel,
        out_shape=jax.ShapeDtypeStruct((ROWS, WIDTH), f32),
        in_specs=[vmem, vmem, hbm, hbm, hbm],
        out_specs=vmem,
        scratch_shapes=[
            pltpu.VMEM((WIDTH, 768), bf16),
            pltpu.VMEM((512, WIDTH), bf16),
            pltpu.VMEM((RING, PAIR, WIDTH), bf16),
            pltpu.VMEM((HEADS_DEV, TOKENS, HEAD_DIM), bf16),
            pltpu.VMEM((TOKENS, HEAD_DIM), bf16),
            pltpu.VMEM((TOKENS, HEAD_DIM), bf16),
            pltpu.VMEM((RING, PAIR, 512), bf16),
            pltpu.VMEM((4, ROWS, WIDTH), f32),
            pltpu.VMEM((4, ROWS, WIDTH), bf16),
            pltpu.VMEM((4, ROWS, WIDTH), bf16),
            pltpu.VMEM((3, ROWS, WIDTH), bf16),
            pltpu.VMEM((2, HALF, WIDTH), bf16),
            pltpu.VMEM((2, ROWS, WIDTH), bf16),
            dma((3,)), dma((2,)), dma((15,)), dma((RING, 2, 2)),
            dma((4,)), dma((4,)), dma((6,)), dma((6,)),
        ],
        compiler_params=pltpu.CompilerParams(
            collective_id=0, has_side_effects=True, vmem_limit_bytes=58 << 20
        ),
        cost_estimate=pl.CostEstimate(flops=12 * 10**9, bytes_accessed=16 << 20, transcendentals=4 << 20),
        name="attention_layer",
    )(x, gain, wq, kv, wo)


def body(
    entry_symbol_ids,
    lookup_table_matrix,
    pending_batches,
    scale_factors,
    query_projector,
    key_projector,
    value_projector,
    result_projector,
):
    pipe_pos = lax.axis_index("pipe")
    tensor_pos = lax.axis_index("tensor")
    section = 2 * (pipe_pos // 2) + tensor_pos % 2
    vocab_dev = lookup_table_matrix.shape[0]
    local_index = entry_symbol_ids - pipe_pos * vocab_dev
    inside = (local_index >= 0) & (local_index < vocab_dev)
    looked = jnp.take(lookup_table_matrix, jnp.clip(local_index, 0, vocab_dev - 1), axis=0)
    looked = jnp.where(inside[:, None], looked, jnp.zeros_like(looked))
    exchanged = lax.all_to_all(
        looked.reshape(8, ROWS, -1), "tensor", split_axis=0, concat_axis=2, tiled=True
    ).reshape(ROWS, WIDTH)
    entering = lax.psum(exchanged.astype(jnp.float32).astype(jnp.bfloat16), "pipe")

    kv = traded(jnp.concatenate([key_projector[0], value_projector[0]], axis=1))
    wq = traded(query_projector[0])
    wo = traded(result_projector[0])
    gain = traded(scale_factors)
    first_in = traded(pending_batches)
    first_out = layer(first_in.astype(jnp.float32), gain, wq, kv, wo)
    passed = to_next_section(first_out)
    second_in = jnp.where(section == 0, traded(entering).astype(jnp.float32), passed)
    second_out = layer(second_in, gain, wq, kv, wo)
    return (traded(first_out), traded(second_out))


def solution(mesh):
    in_specs = (
        P(),
        P("pipe", "tensor"),
        P(("pipe", "tensor"), None),
        P("pipe", None),
        P("pipe", None, "tensor"),
        P("pipe", None, "tensor"),
        P("pipe", None, "tensor"),
        P("pipe", "tensor", None),
    )
    out_specs = (P(("pipe", "tensor"), None), P(("pipe", "tensor"), None))
    return jax.shard_map(body, mesh=mesh, in_specs=in_specs, out_specs=out_specs, check_vma=False)
```

time: 1340 us -> 440 us (0.33)
  waiting for transfers between devices: 1140 us -> 116 us
  Pallas kernels: 0 us -> 192 us
  starting transfers between devices: 4.37 us -> 92.5 us
  matrix products: 87.5 us -> 0 us
  blocking collectives: 38 us -> 0 us
  other arithmetic: 21.4 us -> 4.9 us
    reduce_scatter x2 -> x0, waiting for transfers between devices: 657 us -> none  [shared_key_mixer(): lax.psum_scatter(jnp.dot(context, out_mat, preferred_element_type=jnp.flo...]
    all_gather x2 -> x0, waiting for transfers between devices: 339 us -> none  [shared_key_mixer(): projected = project(lax.all_gather(normed, 'tensor', axis=0, tiled=True))]
    pallas_call x0 -> x2, Pallas kernels: none -> 192 us  [layer(): pl.pallas_call(layer_kernel, out_shape=jax.ShapeDtypeStruct((ROWS, WIDTH)...]
    psum x1, waiting for transfers between devices: 137 us -> 41.6 us  [body(): lax.psum(exchanged.astype(jnp.float32).astype(jnp.bfloat16), 'pipe')]
    all_to_all x0 -> x1, starting transfers between devices: none -> 63.3 us  [body(): lax.all_to_all(looked.reshape(8, ROWS, -1), 'tensor', split_axis=0, conca...]
    dot_general x8 -> x0, matrix products: 62.2 us -> none  [the longest x2 20.8 us: project(): jnp.dot(shard_piece, project_mat, preferred_element_type=jnp.float32)]
    all_to_all x1 -> x0, blocking collectives: 38 us -> none  [body(): lax.all_to_all(looked.reshape(tensor_count, number_lines, -1), 'tensor',...]
    all_to_all x0 -> x1, waiting for transfers between devices: none -> 37 us  [body(): lax.all_to_all(looked.reshape(8, ROWS, -1), 'tensor', split_axis=0, conca...]
  transfers between devices with their start and end apart: 8 -> 11, of which waited for: 7 -> 4; matrix products, arithmetic and copies ran while one was open for 1% -> 4% of each run, Pallas kernels for 0% -> 44%
where the time goes in v1:
time: 440 us; the launch traced here: 434 us
  Pallas kernels  192 us (44%)
  waiting for transfers between devices  116 us (26%)
  starting transfers between devices  92.5 us (21%)
  local copies, waits for them, and re-layouts  15.8 us (4%)
  between operations  14.3 us (3%)
  other arithmetic  4.9 us (1%)
    pallas_call x2, Pallas kernels, layer(): pl.pallas_call(layer_kernel, out_shape=jax.ShapeDtypeStruct((ROWS, WIDTH)...  192 us
    all_to_all x1, starting transfers between devices, body(): lax.all_to_all(looked.reshape(8, ROWS, -1), 'tensor', split_axis=0, conca...  63.3 us
    psum x1, waiting for transfers between devices, body(): lax.psum(exchanged.astype(jnp.float32).astype(jnp.bfloat16), 'pipe')  41.6 us
    all_to_all x1, waiting for transfers between devices, body(): lax.all_to_all(looked.reshape(8, ROWS, -1), 'tensor', split_axis=0, conca...  37 us
    ppermute x8, waiting for transfers between devices, traded(): return lax.ppermute(array, BOTH, route)  36.9 us
    ppermute x8, starting transfers between devices, traded(): return lax.ppermute(array, BOTH, route)  26.1 us
  transfers between devices with their start and end apart: 11, of which 4 were waited for; matrix products, arithmetic and copies ran while one was open for 4% of the time, Pallas kernels for 44%

profile of v1, /device:TPU:1, one launch (start us, length us, event | category | flops | bytes accessed | tf_op | source)
XLA Modules:
  0.0 434.5 jit_solution(11655401123625694898)
XLA Ops:
  7.2 4.9 %collective-permute-start.2 = (bf16[4096,512]{1,0:T(8,128)(2,1)}, bf16[4096,512]{1,0:T(8,128)(2,1)}, u32[]{:S(2)}, u32[]{:S(2)}) collective-permute-start(bf16[4096,512]{1,0:T(8,128)(2,1)} %bitcast.22), channel_id=1, source_target_pairs={{0,0},{1,8},{2,2},{3,10},{4,4},{5,12},{6,6},{7,14},{8,1},{9,9},{10... | collective-permute-start | bytes 12582920 | tf_op jit(solution)/shard_map/ppermute | solution.py:32
  12.1 1.9 collective-permute-start.4
  14.0 1.5 copy.18
  15.6 0.0 copy-start
  15.6 1.6 copy.19
  17.1 0.6 pad_maximum_fusion
  17.7 3.6 collective-permute-start.3
  21.4 1.9 collective-permute-start
  23.3 8.5 %gather_fusion = bf16[1024,512]{1,0:T(8,128)(2,1)S(1)} fusion(bf16[8192,512]{1,0:T(8,128)(2,1)} %param.9, s32[1024]{0:T(1024)S(1)} %fusion), kind=kCustom, calls=%fused_computation | custom fusion | bytes 2101248 | tf_op jit(solution)/shard_map/jit(_take)/gather | solution.py:309
  31.8 0.0 copy-start.1
  31.8 1.2 select_select_fusion
  33.1 63.3 %all-to-all-start = ((bf16[8,128,512]{2,1,0:T(8,128)(2,1)}), bf16[8,128,512]{2,1,0:T(8,128)(2,1)S(1)}, u32[]{:S(2)}, u32[]{:S(2)}) async-start(bf16[8,128,512]{2,1,0:T(8,128)(2,1)} %select_select_fusion), calls=%async_computation | async-start | bytes 2097152 | tf_op jit(solution)/shard_map/all_to_all | solution.py:311
  96.4 0.0 all-reduce.2.cloned.1.call-start
  96.4 3.1 collective-permute-start.1
  99.5 37.0 %all-to-all-done = bf16[8,128,512]{2,1,0:T(8,128)(2,1)S(1)} async-done(((bf16[8,128,512]{2,1,0:T(8,128)(2,1)}), bf16[8,128,512]{2,1,0:T(8,128)(2,1)S(1)}, u32[]{:S(2)}, u32[]{:S(2)}) %all-to-all-start) | async-done | bytes 1048608 | tf_op jit(solution)/shard_map/all_to_all | solution.py:311
  136.5 1.1 copy.21
  137.6 0.0 all-reduce.2.cloned.1.call-update
  137.6 0.0 collective-permute-done
  137.6 1.5 convert_element_type.8.x_ref
  139.2 0.6 copy-done.2
  139.7 97.1 %attention_layer.2 = f32[128,4096]{1,0:T(8,128)} custom-call(f32[128,4096]{1,0:T(8,128)} %convert_element_type.8.x_ref, f32[1,4096]{1,0:T(1,128)} %copy-done.2, bf16[4096,512]{1,0:T(8,128)(2,1)} %collective-permute-done.2.wq_hbm, bf16[4096,128]{1,0:T(8,128)(2,1)} %collective-permute-done.3.kv_hbm, bf16[512,4096]{1,0:T(8,128)(2,1)} %collective-permute-done.4.wo_hbm), custom_call_target="tpu_custom_call" | custom-call | flops 12000000000 | bytes 16777216 | tf_op jit(solution)/shard_map/attention_layer/pallas_call | solution.py:263
  236.9 3.0 collective-permute-start.7
  239.9 41.6 %all-reduce.2.cloned.1.call-done = bf16[128,4096]{1,0:T(8,128)(2,1)} async-done(((bf16[128,4096]{1,0:T(8,128)(2,1)}), bf16[128,4096]{1,0:T(8,128)(2,1)}) %all-reduce.2.cloned.1.call-update) | async-done | bytes 1048592 | tf_op jit(solution)/shard_map/psum | solution.py:314
  281.6 3.3 collective-permute-start.6
  284.9 2.4 collective-permute-start.5
  287.3 12.9 %collective-permute-done.6 = bf16[128,4096]{1,0:T(8,128)(2,1)S(1)} collective-permute-done((bf16[128,4096]{1,0:T(8,128)(2,1)}, bf16[128,4096]{1,0:T(8,128)(2,1)S(1)}, u32[]{:S(2)}, u32[]{:S(2)}) %collective-permute-start.6) | collective-permute-done | bytes 1048608 | tf_op jit(solution)/shard_map/ppermute | solution.py:32
  300.3 1.5 convert_select_fusion.x_ref
  301.8 94.4 %attention_layer.3 = f32[128,4096]{1,0:T(8,128)} custom-call(f32[128,4096]{1,0:T(8,128)} %convert_select_fusion.x_ref, f32[1,4096]{1,0:T(1,128)} %copy-done.2, bf16[4096,512]{1,0:T(8,128)(2,1)} %collective-permute-done.2.wq_hbm, bf16[4096,128]{1,0:T(8,128)(2,1)} %collective-permute-done.3.kv_hbm, bf16[512,4096]{1,0:T(8,128)(2,1)} %collective-permute-done.4.wo_hbm), custom_call_target="tpu_custom_call" | custom-call | flops 12000000000 | bytes 16777216 | tf_op jit(solution)/shard_map/attention_layer/pallas_call | solution.py:263
  396.2 4.9 %collective-permute-start.8 = (f32[128,4096]{1,0:T(8,128)}, f32[128,4096]{1,0:T(8,128)S(1)}, u32[]{:S(2)}, u32[]{:S(2)}) collective-permute-start(f32[128,4096]{1,0:T(8,128)} %attention_layer.3), channel_id=1, source_target_pairs={{0,0},{1,8},{2,2},{3,10},{4,4},{5,12},{6,6},{7,14},{8,1},{9,9},{10... | collective-permute-start | bytes 6291464 | tf_op jit(solution)/shard_map/ppermute | solution.py:32
  401.1 23.9 %collective-permute-done.8 = f32[128,4096]{1,0:T(8,128)S(1)} collective-permute-done((f32[128,4096]{1,0:T(8,128)}, f32[128,4096]{1,0:T(8,128)S(1)}, u32[]{:S(2)}, u32[]{:S(2)}) %collective-permute-start.8) | collective-permute-done | bytes 2097184 | tf_op jit(solution)/shard_map/ppermute | solution.py:32
  425.0 1.3 copy.26
  426.3 1.3 copy.27
  (11 shorter events, 0.0 us)
Async XLA Ops:
  7.2 132.0 %collective-permute-start.2 = (bf16[4096,512]{1,0:T(8,128)(2,1)}, bf16[4096,512]{1,0:T(8,128)(2,1)}, u32[]{:S(2)}, u32[]{:S(2)}) collective-permute-start(bf16[4096,512]{1,0:T(8,128)(2,1)} %bitcast.22), channel_id=1, source_target_pairs={{0,0},{1,8},{2,2},{3,10},{4,4},{5,12},{6,6},{7,14},{8,1},{9,9},{10... | collective-permute-start | bytes 12582920 | tf_op jit(solution)/shard_map/ppermute | solution.py:32
  12.1 127.1 %collective-permute-start.4 = (bf16[512,4096]{1,0:T(8,128)(2,1)}, bf16[512,4096]{1,0:T(8,128)(2,1)}, u32[]{:S(2)}, u32[]{:S(2)}) collective-permute-start(bf16[512,4096]{1,0:T(8,128)(2,1)} %bitcast.23), channel_id=1, source_target_pairs={{0,0},{1,8},{2,2},{3,10},{4,4},{5,12},{6,6},{7,14},{8,1},{9,9},{10... | collective-permute-start | bytes 12582920 | tf_op jit(solution)/shard_map/ppermute | solution.py:32
  15.6 7.8 %copy-start = (s32[1024]{0:T(1024)S(1)}, s32[1024]{0:T(1024)}, u32[]{:S(2)}) copy-start(s32[1024]{0:T(1024)} %param.8) | copy-start | bytes 12292
  17.7 121.4 %collective-permute-start.3 = (bf16[4096,128]{1,0:T(8,128)(2,1)S(1)}, bf16[4096,128]{1,0:T(8,128)(2,1)}, u32[]{:S(2)}, u32[]{:S(2)}) collective-permute-start(bf16[4096,128]{1,0:T(8,128)(2,1)S(1)} %pad_maximum_fusion), channel_id=1, source_target_pairs={{0,0},{1,8},{2,2},{3,10},{4,4},{5,12},{6,6},{7,14},{8,1},{9,9},{10... | collective-permute-start | bytes 3145736 | tf_op jit(solution)/shard_map/ppermute | solution.py:32
  21.4 116.2 %collective-permute-start = (bf16[128,4096]{1,0:T(8,128)(2,1)}, bf16[128,4096]{1,0:T(8,128)(2,1)S(1)}, u32[]{:S(2)}, u32[]{:S(2)}) collective-permute-start(bf16[128,4096]{1,0:T(8,128)(2,1)} %param.10), channel_id=1, source_target_pairs={{0,0},{1,8},{2,2},{3,10},{4,4},{5,12},{6,6},{7,14},{8,1},{9,9},{10... | collective-permute-start | bytes 3145736 | tf_op jit(solution)/shard_map/ppermute | solution.py:32
  31.8 64.6 %copy-start.1 = (f32[1,4096]{1,0:T(1,128)S(1)}, f32[1,4096]{1,0:T(1,128)}, u32[]{:S(2)}) copy-start(f32[1,4096]{1,0:T(1,128)} %param.11) | copy-start | bytes 49156
  33.1 103.4 %all-to-all-start = ((bf16[8,128,512]{2,1,0:T(8,128)(2,1)}), bf16[8,128,512]{2,1,0:T(8,128)(2,1)S(1)}, u32[]{:S(2)}, u32[]{:S(2)}) async-start(bf16[8,128,512]{2,1,0:T(8,128)(2,1)} %select_select_fusion), calls=%async_computation | async-start | bytes 2097152 | tf_op jit(solution)/shard_map/all_to_all | solution.py:311
  96.4 185.2 %all-reduce.2.cloned.1.call-start = ((), (), s32[]{:S(2)}) async-start(), calls=%async_computation.1 | async-start | bytes 2097152 | tf_op jit(solution)/shard_map/psum | solution.py:314
  96.4 42.7 %collective-permute-start.1 = (f32[1,4096]{1,0:T(1,128)S(1)}, f32[1,4096]{1,0:T(1,128)S(1)}, u32[]{:S(2)}, u32[]{:S(2)}) collective-permute-start(f32[1,4096]{1,0:T(1,128)S(1)} %copy-done.1), channel_id=1, source_target_pairs={{0,0},{1,8},{2,2},{3,10},{4,4},{5,12},{6,6},{7,14},{8,1},{9,9},{10... | collective-permute-start | bytes 49160 | tf_op jit(solution)/shard_map/ppermute | solution.py:32
  139.1 0.6 copy-start.2
  236.9 63.4 %collective-permute-start.7 = (f32[128,4096]{1,0:T(8,128)}, f32[128,4096]{1,0:T(8,128)S(1)}, u32[]{:S(2)}, u32[]{:S(2)}) collective-permute-start(f32[128,4096]{1,0:T(8,128)} %attention_layer.2), channel_id=1, source_target_pairs={{0,1},{8,9},{2,3},{10,11},{4,5},{12,13},{6,7},{14,15},{1,16},{9,24... | collective-permute-start | bytes 6291464 | tf_op jit(solution)/shard_map/ppermute | solution.py:37
  281.6 18.7 %collective-permute-start.6 = (bf16[128,4096]{1,0:T(8,128)(2,1)}, bf16[128,4096]{1,0:T(8,128)(2,1)S(1)}, u32[]{:S(2)}, u32[]{:S(2)}) collective-permute-start(bf16[128,4096]{1,0:T(8,128)(2,1)} %all-reduce.2.cloned.1.call-done), channel_id=1, source_target_pairs={{0,0},{1,8},{2,2},{3,10},{4,4},{5,12},{6,6},{7,14},{8,1},{9,9},{10... | collective-permute-start | bytes 3145736 | tf_op jit(solution)/shard_map/ppermute | solution.py:32
  284.9 116.2 %collective-permute-start.5 = (f32[128,4096]{1,0:T(8,128)}, f32[128,4096]{1,0:T(8,128)S(1)}, u32[]{:S(2)}, u32[]{:S(2)}) collective-permute-start(f32[128,4096]{1,0:T(8,128)} %attention_layer.2), channel_id=1, source_target_pairs={{0,0},{1,8},{2,2},{3,10},{4,4},{5,12},{6,6},{7,14},{8,1},{9,9},{10... | collective-permute-start | bytes 6291464 | tf_op jit(solution)/shard_map/ppermute | solution.py:32
  396.2 28.8 %collective-permute-start.8 = (f32[128,4096]{1,0:T(8,128)}, f32[128,4096]{1,0:T(8,128)S(1)}, u32[]{:S(2)}, u32[]{:S(2)}) collective-permute-start(f32[128,4096]{1,0:T(8,128)} %attention_layer.3), channel_id=1, source_target_pairs={{0,0},{1,8},{2,2},{3,10},{4,4},{5,12},{6,6},{7,14},{8,1},{9,9},{10... | collective-permute-start | bytes 6291464 | tf_op jit(solution)/shard_map/ppermute | solution.py:32
Sparse Core Ops, SparseCore 0:
  137.7 143.8 all-reduce.1

commit v2 on v1

v2 whole, which is shorter than its diff:
```python
import functools

import jax
import jax.numpy as jnp
from jax import lax
from jax.experimental import pallas as pl
from jax.experimental.pallas import tpu as pltpu
from jax.sharding import PartitionSpec as P

HEAD_DIM = 128
MESH = pl.DeviceIdType.MESH
BOTH = ("pipe", "tensor")
SECTIONS = 16
RING = 4
TOKENS = 1024
ROWS = 128
WIDTH = 4096
COLS = 512
HEADS_DEV = 4
PAIR = 2 * ROWS
HALF = ROWS // 2
PARTS = 8
PART = WIDTH // PARTS


def flat(pipe, tensor):
    return pipe * 8 + tensor


def physical(section, block):
    return flat(2 * (section // 2) + block % 2, 2 * (block // 2) + section % 2)


def traded(array):
    route = [(flat(s, t), physical(s, t)) for s in range(SECTIONS) for t in range(8)]
    return lax.ppermute(array, BOTH, route)


def remote(src, dst, send_sem, recv_sem, device):
    return pltpu.make_async_remote_copy(
        src_ref=src, dst_ref=dst, send_sem=send_sem, recv_sem=recv_sem,
        device_id=device, device_id_type=MESH,
    )


def aligned(start, size):
    return pl.ds(pl.multiple_of(start, size), size)


def layer_kernel(first, *refs):
    if first:
        (x_ref, gain_ref, wq_hbm, kv_hbm, wo_hbm, looked_hbm,
         out_hbm, next_hbm, w_in_hbm, w_out_hbm, *refs) = refs
    else:
        (x_ref, gain_ref, w_in_hbm, w_out_hbm, held_hbm, held_out, out_hbm, *refs) = refs
    (w_in, w_out, normed, q_s, k_s, v_s, ctx, own_part, sib_out, sib_in, ring_out, relay, arrived,
     out_s, load_sem, kv_sem, ag_send, ag_recv, sib_send, sib_recv, ring_send, ring_recv,
     trade_send, trade_recv, out_send, out_recv, *refs) = refs
    if first:
        next_s, e_acc, e_in, e_sem, e_send, e_recv, all_send, all_recv, next_send, next_recv = refs

    pipe = lax.axis_index("pipe")
    tensor = lax.axis_index("tensor")
    core = lax.rem(pipe, 2)
    x_pos = lax.rem(lax.div(pipe, 2), 4)
    z_hi = lax.div(pipe, 8)
    y = lax.div(tensor, 2)
    z_lo = lax.rem(tensor, 2)
    y_up = lax.rem(y + 1, RING)
    y_far = lax.rem(y + 2, RING)
    y_down = lax.rem(y + 3, RING)
    other = 1 - core
    section = pipe - core + z_lo
    sibling = (pipe + 1 - 2 * core, tensor)
    up = (pipe, 2 * y_up + z_lo)
    down = (pipe, 2 * y_down + z_lo)
    stays = core == z_lo
    moves = core != z_lo
    partner = (pipe - core + z_lo, tensor - z_lo + core)
    has_next = section < SECTIONS - 1
    has_prev = section > 0
    after = (pipe + 2 * z_lo, tensor + 1 - 2 * z_lo)
    before = (pipe - 2 * (1 - z_lo), tensor + 1 - 2 * z_lo)

    barrier = pltpu.get_barrier_semaphore()
    greeted = []

    def greet(device, condition=None):
        def signal():
            pl.semaphore_signal(barrier, inc=1, device_id=device, device_id_type=MESH)

        if condition is None:
            signal()
            greeted.append(1)
        else:
            pl.when(condition)(signal)
            greeted.append(jnp.where(condition, 1, 0))

    greet(sibling)
    greet(up)
    greet(down)
    greet(partner, moves)
    if first:
        lead = core == 0
        x_odd = lax.rem(x_pos, 2) == 1
        sends_2 = lead & x_odd
        takes_2 = lead & (lax.rem(x_pos, 2) == 0)
        sends_3 = lead & (x_pos == 2)
        takes_3 = lead & (x_pos == 0)
        sends_4 = lead & (x_pos == 0) & (z_hi == 1)
        is_root = pipe == 0
        enters = (section == 0)
        greet(after, has_next)
        greet(before, has_prev)
        greet((pipe - 2, tensor), sends_2)
        greet((pipe + 2, tensor), takes_2)
        greet((pipe - 4, tensor), sends_3)
        greet((pipe + 4, tensor), takes_3)
        greet((pipe - 8, tensor), sends_4)
        greet((pipe + 8, tensor), is_root)
        for t in range(8):
            is_me = (pipe == t % 2) & (tensor == 2 * (t // 2))
            greet((t % 2, 2 * (t // 2)), is_root & jnp.logical_not(is_me))
            greet((0, t), enters & jnp.logical_not(is_root & (tensor == t)))
        load_looked = pltpu.make_async_copy(looked_hbm, e_acc, e_sem.at[0])
        load_looked.start()
    else:
        load_in = pltpu.make_async_copy(w_in_hbm, w_in, load_sem.at[0])
        load_in.start()
        load_out = pltpu.make_async_copy(w_out_hbm, w_out, load_sem.at[1])
        load_out.start()

    def norm_rows(step, carry):
        x = x_ref[aligned(step * 16, 16), :].astype(jnp.float32)
        scale = lax.rsqrt(jnp.mean(x * x, axis=1, keepdims=True) + 1e-05)
        normed[y, aligned(core * ROWS + step * 16, 16), :] = (x * scale * gain_ref[...]).astype(jnp.bfloat16)
        return carry

    lax.fori_loop(0, ROWS // 16, norm_rows, 0)
    pl.semaphore_wait(barrier, functools.reduce(lambda a, b: a + b, greeted))

    def hand_over(src, dst, slot, sends=trade_send, recvs=trade_recv):
        @pl.when(stays)
        def _():
            pltpu.make_async_copy(src, dst, recvs.at[slot]).start()

        @pl.when(moves)
        def _():
            remote(src, dst, sends.at[slot], recvs.at[slot], partner).start()

    def handed(src, dst, slot, sends=trade_send, recvs=trade_recv):
        remote(src, dst, sends.at[slot], recvs.at[slot], partner).wait_recv()

    def handed_over(src, dst, slot, sends=trade_send, recvs=trade_recv):
        @pl.when(moves)
        def _():
            remote(src, dst, sends.at[slot], recvs.at[slot], partner).wait_send()

    sends = []

    def piece(chip, side, half):
        return normed.at[chip, aligned(side * ROWS + half * HALF, HALF), :]

    def gather(chip, side, half, device):
        part = piece(chip, side, half)
        copy = remote(part, part, ag_send.at[len(sends)], ag_recv.at[chip, side, half], device)
        copy.start()
        sends.append(copy)

    def wait_piece(chip, side, half):
        part = piece(chip, side, half)
        remote(part, part, ag_send.at[0], ag_recv.at[chip, side, half], sibling).wait_recv()

    gather(y, core, 0, up)
    gather(y, core, 1, down)
    gather(y, core, 0, sibling)
    gather(y, core, 1, sibling)
    gather(y, core, 1, up)
    gather(y, core, 0, down)

    def forward_near():
        wait_piece(y_down, core, 0)
        gather(y_down, core, 0, up)
        gather(y_down, core, 0, sibling)
        wait_piece(y_up, core, 1)
        gather(y_up, core, 1, down)
        gather(y_up, core, 1, sibling)
        wait_piece(y_down, core, 1)
        gather(y_down, core, 1, sibling)
        wait_piece(y_up, core, 0)
        gather(y_up, core, 0, sibling)

    def forward_far():
        wait_piece(y_far, core, 0)
        gather(y_far, core, 0, sibling)
        wait_piece(y_far, core, 1)
        gather(y_far, core, 1, sibling)

    def project(chip):
        rows = aligned(chip * PAIR, PAIR)

        def two_heads(n, carry):
            res = jnp.dot(normed[chip], w_in[:, aligned(n * 256, 256)], preferred_element_type=jnp.float32)
            q_s[2 * n, rows, :] = res[:, :128].astype(jnp.bfloat16)
            q_s[2 * n + 1, rows, :] = res[:, 128:].astype(jnp.bfloat16)
            return carry

        lax.fori_loop(0, 2, two_heads, 0)
        res = jnp.dot(normed[chip], w_in[:, 512:768], preferred_element_type=jnp.float32)
        k_s[rows, :] = jnp.concatenate([res[:, 0:64], res[:, 128:192]], axis=1).astype(jnp.bfloat16)
        v_s[rows, :] = jnp.concatenate([res[:, 64:128], res[:, 192:256]], axis=1).astype(jnp.bfloat16)

    def out_cols(n):
        return aligned(n * PART, PART)

    if first:
        kv_own = w_in.at[:, aligned(512 + core * 128, 128)]
        kv_partner = w_in.at[:, aligned(512 + z_lo * 128, 128)]
        kv_rest = w_in.at[:, aligned(512 + other * 128, 128)]
        wq_slot = w_in.at[:, pl.ds(0, 512)]

        def wo_part(n):
            return (wo_hbm.at[:, out_cols(n)], w_out.at[:, out_cols(n)], 2 + n)

        hand_over(kv_hbm, kv_partner, 0)
        hand_over(wq_hbm, wq_slot, 1)

        def tree(slot, src, device):
            return remote(src, e_in.at[slot], e_send.at[slot], e_recv.at[slot], device)

        def add_in(slot):
            tree(slot, e_acc, sibling).wait_recv()

            def rows_step(step, carry):
                rows = aligned(step * 64, 64)
                e_acc[rows, :] = e_acc[rows, :] + e_in[slot, rows, :]
                return carry

            lax.fori_loop(0, TOKENS // 64, rows_step, 0)

        load_looked.wait()

        @pl.when(core == 1)
        def _():
            tree(0, e_acc, sibling).start()

        @pl.when(lead)
        def _():
            add_in(0)

        @pl.when(sends_2)
        def _():
            tree(1, e_acc, (pipe - 2, tensor)).start()

        forward_near()

        @pl.when(takes_2)
        def _():
            add_in(1)

        @pl.when(sends_3)
        def _():
            tree(2, e_acc, (pipe - 4, tensor)).start()

        forward_far()

        @pl.when(takes_3)
        def _():
            add_in(2)

        @pl.when(sends_4)
        def _():
            tree(3, e_acc, (pipe - 8, tensor)).start()

        handed(kv_hbm, kv_own, 0)
        share = remote(kv_own, kv_own, kv_sem.at[0], kv_sem.at[1], sibling)
        share.start()
        handed(wq_hbm, wq_slot, 1)
        handed_over(kv_hbm, kv_partner, 0)
        handed_over(wq_hbm, wq_slot, 1)
        for n in range(2):
            hand_over(*wo_part(n))
        remote(kv_rest, kv_rest, kv_sem.at[0], kv_sem.at[1], sibling).wait_recv()
        keep_in = pltpu.make_async_copy(w_in, w_in_hbm, load_sem.at[0])
        keep_in.start()
        for chip in range(RING):
            for side in range(2):
                @pl.when((side != core) | False)
                def _(chip=chip, side=side):
                    wait_piece(chip, side, 0)
                    wait_piece(chip, side, 1)

        def project_step(chip, carry):
            project(chip)
            return carry

        lax.fori_loop(0, RING, project_step, 0)
    else:
        held_src = held_hbm
        hand_over(held_src, held_out, 0)
        wait_piece(y, other, 0)
        wait_piece(y, other, 1)
        load_in.wait()
        project(y)
        forward_near()
        for chip in (y_down, y_up):
            wait_piece(chip, other, 0)
            wait_piece(chip, other, 1)
            project(chip)
        forward_far()
        wait_piece(y_far, other, 0)
        wait_piece(y_far, other, 1)
        project(y_far)

    scale = HEAD_DIM ** (-0.5)

    def head(h, carry):
        cols = aligned(h * HEAD_DIM, HEAD_DIM)
        for i in range(RING):
            keys = PAIR * (i + 1)
            scores = lax.dot_general(
                q_s[h, PAIR * i : keys, :], k_s[:keys, :], (((1,), (1,)), ((), ())),
                preferred_element_type=jnp.float32,
            ) * scale
            q_pos = PAIR * i + lax.broadcasted_iota(jnp.int32, (PAIR, keys), 0)
            k_pos = lax.broadcasted_iota(jnp.int32, (PAIR, keys), 1)
            scores = jnp.where(q_pos >= k_pos, scores, -1e30)
            top = jnp.max(scores, axis=1, keepdims=True)
            exps = jnp.exp(scores - top)
            weights = (exps * (1.0 / jnp.sum(exps, axis=1, keepdims=True))).astype(jnp.bfloat16)
            mixed = jnp.dot(weights, v_s[:keys, :], preferred_element_type=jnp.float32)
            ctx[i, :, cols] = mixed.astype(jnp.bfloat16)
        return carry

    lax.fori_loop(0, HEADS_DEV, head, 0)

    if first:
        def spread(t, column):
            return (
                e_acc.at[pl.ds(t * ROWS, ROWS), :],
                next_hbm.at[:, aligned(column * COLS, COLS)],
            )

        @pl.when(is_root)
        def _():
            add_in(3)
            for t in range(8):
                src, dst = spread(t, tensor)
                is_me = (t % 2 == 0) & (tensor == 2 * (t // 2))

                @pl.when(is_me)
                def _(src=src, dst=dst):
                    pltpu.make_async_copy(src, dst, all_recv.at[tensor]).start()

                @pl.when(jnp.logical_not(is_me))
                def _(src=src, dst=dst, t=t):
                    remote(src, dst, all_send.at[t], all_recv.at[tensor], (t % 2, 2 * (t // 2))).start()

    def sib_copy(n):
        return remote(sib_out.at[n], sib_in.at[n], sib_send.at[n], sib_recv.at[n], sibling)

    low, high = pl.ds(0, HALF), pl.ds(HALF, HALF)
    ring_plan = (
        (0, low, "relay", 0, up),
        (0, high, "relay", 1, down),
        (1, high, "arrived", 0, up),
        (2, low, "arrived", 1, down),
        (1, low, "arrived", 0, up),
        (2, high, "arrived", 1, down),
    )

    def ring_copy(n, index):
        slot, rows, into, side, device = ring_plan[index]
        dst = relay.at[n, side] if into == "relay" else arrived.at[n, side, rows]
        return remote(ring_out.at[n, slot, rows], dst, ring_send.at[n, index], ring_recv.at[n, index], device)

    def combine(n, slot, ring_slot, first_row, count, relayed):
        def rows_step(step, carry):
            rows = aligned(first_row + step * 16, 16)
            total = own_part[n, slot, rows, :] + sib_in[n, slot, rows, :].astype(jnp.float32)
            if relayed is not None:
                total = total + relay[n, relayed, aligned(step * 16, 16), :].astype(jnp.float32)
            ring_out[n, ring_slot, rows, :] = total.astype(jnp.bfloat16)
            return carry

        lax.fori_loop(0, count // 16, rows_step, 0)

    def project_part(n):
        if first:
            handed(*wo_part(n))
            handed_over(*wo_part(n))

            @pl.when(n < PARTS - 2)
            def _():
                hand_over(*wo_part(n + 2))

        def slot_step(slot, carry):
            chip = lax.rem(y + 6 - slot, RING)
            res = jnp.dot(ctx[chip], w_out[:, out_cols(n)], preferred_element_type=jnp.float32)
            top, bottom = res[:ROWS], res[ROWS:]
            own_part[n, slot] = jnp.where(core == 0, top, bottom)
            sib_out[n, slot] = jnp.where(core == 0, bottom, top).astype(jnp.bfloat16)
            return carry

        lax.fori_loop(0, 4, slot_step, 0)
        sib_copy(n).start()

    def send_part(n):
        sib_copy(n).wait_recv()
        combine(n, 0, 0, 0, ROWS, None)
        ring_copy(n, 0).start()
        ring_copy(n, 1).start()
        combine(n, 1, 1, HALF, HALF, None)
        ring_copy(n, 2).start()
        combine(n, 3, 2, 0, HALF, None)
        ring_copy(n, 3).start()

    def relay_part(n):
        ring_copy(n, 0).wait_recv()
        combine(n, 1, 1, 0, HALF, 0)
        ring_copy(n, 4).start()
        ring_copy(n, 1).wait_recv()
        combine(n, 3, 2, HALF, HALF, 1)
        ring_copy(n, 5).start()

    def next_copy(n, device):
        return remote(next_s.at[n], next_hbm.at[:, out_cols(n)], next_send.at[n], next_recv.at[n], device)

    def out_part(n):
        return (out_s.at[n], out_hbm.at[:, out_cols(n)], n)

    def finish_part(n):
        for index in (2, 3, 4, 5):
            ring_copy(n, index).wait_recv()

        def rows_step(step, carry):
            rows = aligned(step * 16, 16)
            total = own_part[n, 2, rows, :] + sib_in[n, 2, rows, :].astype(jnp.float32)
            total = total + arrived[n, 0, rows, :].astype(jnp.float32)
            total = total + arrived[n, 1, rows, :].astype(jnp.float32)
            total = x_ref[rows, out_cols(n)].astype(jnp.float32) + total
            out_s[n, rows, :] = total
            if first:
                next_s[n, rows, :] = total.astype(jnp.bfloat16)
            return carry

        lax.fori_loop(0, ROWS // 16, rows_step, 0)
        if first:
            @pl.when(has_next)
            def _():
                next_copy(n, after).start()

            pltpu.make_async_copy(out_s.at[n], out_hbm.at[:, out_cols(n)], out_recv.at[n]).start()
        else:
            hand_over(*out_part(n), out_send, out_recv)

    if not first:
        load_out.wait()

    def pipeline(i, carry):
        @pl.when(i < PARTS)
        def _():
            project_part(i)

        @pl.when((i >= 1) & (i < PARTS + 1))
        def _():
            send_part(i - 1)

        @pl.when((i >= 2) & (i < PARTS + 2))
        def _():
            relay_part(i - 2)

        @pl.when(i >= 3)
        def _():
            finish_part(i - 3)

        return carry

    lax.fori_loop(0, PARTS + 3, pipeline, 0)

    if first:
        keep_out = pltpu.make_async_copy(w_out, w_out_hbm, load_sem.at[1])
        keep_out.start()
        share.wait_send()
        keep_in.wait()
        keep_out.wait()

        @pl.when(core == 1)
        def _():
            tree(0, e_acc, sibling).wait_send()

        @pl.when(sends_2)
        def _():
            tree(1, e_acc, (pipe - 2, tensor)).wait_send()

        @pl.when(sends_3)
        def _():
            tree(2, e_acc, (pipe - 4, tensor)).wait_send()

        @pl.when(sends_4)
        def _():
            tree(3, e_acc, (pipe - 8, tensor)).wait_send()

        @pl.when(is_root)
        def _():
            for t in range(8):
                src, dst = spread(t, tensor)

                @pl.when(jnp.logical_not((t % 2 == 0) & (tensor == 2 * (t // 2))))
                def _(src=src, dst=dst, t=t):
                    remote(src, dst, all_send.at[t], all_recv.at[tensor], (t % 2, 2 * (t // 2))).wait_send()

        @pl.when(enters)
        def _():
            for t in range(8):
                src, dst = spread(0, t)
                remote(src, dst, all_send.at[0], all_recv.at[t], sibling).wait_recv()

    else:
        handed(held_src, held_out, 0)
        handed_over(held_src, held_out, 0)

    for copy in sends:
        copy.wait_send()

    def drain(n, carry):
        sib_copy(n).wait_send()
        for index in range(6):
            ring_copy(n, index).wait_send()
        if first:
            @pl.when(has_next)
            def _():
                next_copy(n, after).wait_send()

            @pl.when(has_prev)
            def _():
                next_copy(n, after).wait_recv()

            pltpu.make_async_copy(out_s.at[n], out_hbm.at[:, out_cols(n)], out_recv.at[n]).wait()
        else:
            handed(*out_part(n), out_send, out_recv)
            handed_over(*out_part(n), out_send, out_recv)
        return carry

    lax.fori_loop(0, PARTS, drain, 0)


def layer(first, *operands):
    bf16, f32 = jnp.bfloat16, jnp.float32
    dma = pltpu.SemaphoreType.DMA
    vmem = pl.BlockSpec(memory_space=pltpu.VMEM)
    hbm = pl.BlockSpec(memory_space=pl.ANY)
    block = jax.ShapeDtypeStruct((ROWS, WIDTH), f32)
    if first:
        out_shape = (
            block,
            jax.ShapeDtypeStruct((ROWS, WIDTH), bf16),
            jax.ShapeDtypeStruct((WIDTH, 768), bf16),
            jax.ShapeDtypeStruct((512, WIDTH), bf16),
        )
    else:
        out_shape = (block, block)
    scratch = [
        pltpu.VMEM((WIDTH, 768), bf16),
        pltpu.VMEM((512, WIDTH), bf16),
        pltpu.VMEM((RING, PAIR, WIDTH), bf16),
        pltpu.VMEM((HEADS_DEV, TOKENS, HEAD_DIM), bf16),
        pltpu.VMEM((TOKENS, HEAD_DIM), bf16),
        pltpu.VMEM((TOKENS, HEAD_DIM), bf16),
        pltpu.VMEM((RING, PAIR, 512), bf16),
        pltpu.VMEM((PARTS, 4, ROWS, PART), f32),
        pltpu.VMEM((PARTS, 4, ROWS, PART), bf16),
        pltpu.VMEM((PARTS, 4, ROWS, PART), bf16),
        pltpu.VMEM((PARTS, 3, ROWS, PART), bf16),
        pltpu.VMEM((PARTS, 2, HALF, PART), bf16),
        pltpu.VMEM((PARTS, 2, ROWS, PART), bf16),
        pltpu.VMEM((PARTS, ROWS, PART), f32),
        dma((2,)), dma((2,)), dma((14,)), dma((RING, 2, 2)),
        dma((PARTS,)), dma((PARTS,)), dma((PARTS, 6)), dma((PARTS, 6)),
        dma((2 + PARTS,)), dma((2 + PARTS,)), dma((PARTS,)), dma((PARTS,)),
    ]
    if first:
        scratch += [
            pltpu.VMEM((PARTS, ROWS, PART), bf16),
            pltpu.VMEM((TOKENS, COLS), bf16),
            pltpu.VMEM((4, TOKENS, COLS), bf16),
            dma((1,)), dma((4,)), dma((4,)), dma((8,)), dma((8,)), dma((PARTS,)), dma((PARTS,)),
        ]
    return pl.pallas_call(
        functools.partial(layer_kernel, first),
        out_shape=out_shape,
        in_specs=[vmem, vmem] + [hbm] * (len(operands) - 2),
        out_specs=tuple(hbm for _ in out_shape),
        scratch_shapes=scratch,
        compiler_params=pltpu.CompilerParams(
            collective_id=0 if first else 1, has_side_effects=True, vmem_limit_bytes=60 << 20
        ),
        cost_estimate=pl.CostEstimate(flops=12 * 10**9, bytes_accessed=16 << 20, transcendentals=4 << 20),
        name="first_layer" if first else "second_layer",
    )(*operands)


def body(
    entry_symbol_ids,
    lookup_table_matrix,
    pending_batches,
    scale_factors,
    query_projector,
    key_projector,
    value_projector,
    result_projector,
):
    pipe_pos = lax.axis_index("pipe")
    vocab_dev = lookup_table_matrix.shape[0]
    local_index = entry_symbol_ids - pipe_pos * vocab_dev
    inside = (local_index >= 0) & (local_index < vocab_dev)
    looked = jnp.take(lookup_table_matrix, jnp.clip(local_index, 0, vocab_dev - 1), axis=0)
    looked = jnp.where(inside[:, None], looked, jnp.zeros_like(looked))
    kv = jnp.concatenate([key_projector[0], value_projector[0]], axis=1)
    gain = traded(scale_factors)
    first_in = traded(pending_batches)
    first_held, second_in, w_in, w_out = layer(
        True, first_in, gain, query_projector[0], kv, result_projector[0], looked
    )
    return layer(False, second_in, gain, w_in, w_out, first_held)


def solution(mesh):
    in_specs = (
        P(),
        P("pipe", "tensor"),
        P(("pipe", "tensor"), None),
        P("pipe", None),
        P("pipe", None, "tensor"),
        P("pipe", None, "tensor"),
        P("pipe", None, "tensor"),
        P("pipe", "tensor", None),
    )
    out_specs = (P(("pipe", "tensor"), None), P(("pipe", "tensor"), None))
    return jax.shard_map(body, mesh=mesh, in_specs=in_specs, out_specs=out_specs, check_vma=False)
```

time: 440 us -> 287 us (0.65)
  waiting for transfers between devices: 116 us -> 0.01 us
  starting transfers between devices: 92.5 us -> 6.86 us
  Pallas kernels: 192 us -> 257 us
  between operations: 14.3 us -> 0.73 us
    pallas_call x2, Pallas kernels: 192 us -> 257 us  [layer(): pl.pallas_call(functools.partial(layer_kernel, first), out_shape=out_shap...]
    all_to_all x1 -> x0, starting transfers between devices: 63.3 us -> none  [body(): lax.all_to_all(looked.reshape(8, ROWS, -1), 'tensor', split_axis=0, conca...]
    psum x1 -> x0, waiting for transfers between devices: 41.6 us -> none  [body(): lax.psum(exchanged.astype(jnp.float32).astype(jnp.bfloat16), 'pipe')]
    all_to_all x1 -> x0, waiting for transfers between devices: 37 us -> none  [body(): lax.all_to_all(looked.reshape(8, ROWS, -1), 'tensor', split_axis=0, conca...]
    ppermute x8 -> x2, waiting for transfers between devices: 36.9 us -> 0.01 us  [traded(): return lax.ppermute(array, BOTH, route)]
    ppermute x8 -> x2, starting transfers between devices: 26.1 us -> 6.86 us  [traded(): return lax.ppermute(array, BOTH, route)]
  transfers between devices with their start and end apart: 11 -> 2, of which waited for: 4 -> 0; matrix products, arithmetic and copies ran while one was open for 4% -> 5% of each run, Pallas kernels for 44% -> 0%
where the time goes in v2:
time: 287 us; the launch traced here: 285 us
  Pallas kernels  257 us (90%)
  local copies, waits for them, and re-layouts  16.7 us (6%)
  starting transfers between devices  6.86 us (2%)
  other arithmetic  3.83 us (1%)
    pallas_call x2, Pallas kernels, layer(): pl.pallas_call(functools.partial(layer_kernel, first), out_shape=out_shap...  257 us
    gather x1, local copies, waits for them, and re-layouts, body(): jnp.take(lookup_table_matrix, jnp.clip(local_index, 0, vocab_dev - 1), ax...  8.46 us
    unnamed x10, local copies, waits for them, and re-layouts  8.22 us
    ppermute x2, starting transfers between devices, traded(): return lax.ppermute(array, BOTH, route)  6.86 us
  transfers between devices with their start and end apart: 2, of which 0 were waited for; matrix products, arithmetic and copies ran while one was open for 5% of the time, Pallas kernels for 0%

profile of v2, /device:TPU:1, one launch (start us, length us, event | category | flops | bytes accessed | tf_op | source)
XLA Modules:
  0.0 285.3 jit_solution(13934848108467736959)
XLA Ops:
  0.6 4.9 %collective-permute-start.1 = (f32[1,4096]{1,0:T(1,128)}, f32[1,4096]{1,0:T(1,128)S(1)}, u32[]{:S(2)}, u32[]{:S(2)}) collective-permute-start(f32[1,4096]{1,0:T(1,128)} %param.11), channel_id=1, source_target_pairs={{0,0},{1,8},{2,2},{3,10},{4,4},{5,12},{6,6},{7,14},{8,1},{9,9},{10... | collective-permute-start | bytes 49160 | tf_op jit(solution)/shard_map/ppermute | solution.py:36
  5.6 1.9 collective-permute-start
  7.5 0.7 fusion
  8.2 1.5 copy.10
  9.7 1.5 copy.11
  11.3 0.0 copy-start.1
  11.3 8.5 %gather_fusion = bf16[1024,512]{1,0:T(8,128)(2,1)S(1)} fusion(bf16[8192,512]{1,0:T(8,128)(2,1)} %param.9, s32[1024]{0:T(1024)S(1)} %fusion), kind=kCustom, calls=%fused_computation | custom fusion | bytes 2101248 | tf_op jit(solution)/shard_map/jit(_take)/gather | solution.py:617
  19.7 0.0 copy-done.1
  19.8 1.5 pad_maximum_fusion.refs_3_
  21.3 1.6 select_select_fusion.refs_5_
  22.9 0.0 collective-permute-done.1.refs_1_
  22.9 0.0 copy-start.2
  22.9 0.0 collective-permute-done.refs_0_
  22.9 0.6 copy-done.2
  23.5 155.4 %first_layer.1 = (f32[128,4096]{1,0:T(8,128)}, bf16[128,4096]{1,0:T(8,128)(2,1)}, bf16[4096,768]{1,0:T(8,128)(2,1)}, bf16[512,4096]{1,0:T(8,128)(2,1)}) custom-call(bf16[128,4096]{1,0:T(8,128)(2,1)} %collective-permute-done.refs_0_, f32[1,4096]{1,0:T(1,128)} %copy-done.2, bf16[4096,512]{1,0:T(8,128)(2,1)} %bitcast.6, ...), custom_call_target="tpu_custom_call" | custom-call | flops 12000000000 | bytes 16777216 | tf_op jit(solution)/shard_map/first_layer/pallas_call | solution.py:589
  178.9 101.8 %second_layer.1 = (f32[128,4096]{1,0:T(8,128)}, f32[128,4096]{1,0:T(8,128)}) custom-call(bf16[128,4096]{1,0:T(8,128)(2,1)} %get-tuple-element.6.refs_0_, f32[1,4096]{1,0:T(1,128)} %copy-done.2, bf16[4096,768]{1,0:T(8,128)(2,1)} %get-tuple-element.7.refs_2_, bf16[512,4096]{1,0:T(8,128)(2,1)} %get-tuple-element.8.refs_3_, f32[128,4096]{1,0:T(8,128)} %get-tuple-element.9.refs_4_), custom_call_target="tpu_custom_call" | custom-call | flops 12000000000 | bytes 16777216 | tf_op jit(solution)/shard_map/second_layer/pallas_call | solution.py:589
  280.7 0.0 copy-start
  280.7 3.3 %copy.14 = f32[128,4096]{1,0:T(8,128)} copy(f32[128,4096]{1,0:T(8,128)} %get-tuple-element.14) | data formatting | bytes 4194304
  284.0 0.0 copy-done
  284.0 1.3 copy.15
  (1 shorter events, 0.0 us)
Async XLA Ops:
  0.6 22.3 %collective-permute-start.1 = (f32[1,4096]{1,0:T(1,128)}, f32[1,4096]{1,0:T(1,128)S(1)}, u32[]{:S(2)}, u32[]{:S(2)}) collective-permute-start(f32[1,4096]{1,0:T(1,128)} %param.11), channel_id=1, source_target_pairs={{0,0},{1,8},{2,2},{3,10},{4,4},{5,12},{6,6},{7,14},{8,1},{9,9},{10... | collective-permute-start | bytes 49160 | tf_op jit(solution)/shard_map/ppermute | solution.py:36
  5.6 17.3 %collective-permute-start = (bf16[128,4096]{1,0:T(8,128)(2,1)}, bf16[128,4096]{1,0:T(8,128)(2,1)}, u32[]{:S(2)}, u32[]{:S(2)}) collective-permute-start(bf16[128,4096]{1,0:T(8,128)(2,1)} %param.10), channel_id=1, source_target_pairs={{0,0},{1,8},{2,2},{3,10},{4,4},{5,12},{6,6},{7,14},{8,1},{9,9},{10... | collective-permute-start | bytes 3145736 | tf_op jit(solution)/shard_map/ppermute | solution.py:36
  11.3 8.5 %copy-start.1 = (s32[1024]{0:T(1024)S(1)}, s32[1024]{0:T(1024)}, u32[]{:S(2)}) copy-start(s32[1024]{0:T(1024)} %param.8) | copy-start | bytes 12292
  22.9 0.6 copy-start.2
  280.7 3.3 %copy-start = (f32[128,4096]{1,0:T(8,128)S(1)}, f32[128,4096]{1,0:T(8,128)}, u32[]{:S(2)}) copy-start(f32[128,4096]{1,0:T(8,128)} %get-tuple-element.15) | copy-start | bytes 6291460

commit v3 on v2

--- a/solution.py
+++ b/solution.py
@@ -21,6 +21,7 @@
 HALF = ROWS // 2
 PARTS = 8
 PART = WIDTH // PARTS
+AHEAD = 3
 
 
 def flat(pipe, tensor):
@@ -31,9 +32,9 @@
     return flat(2 * (section // 2) + block % 2, 2 * (block // 2) + section % 2)
 
 
-def traded(array):
+def from_partner(array):
     route = [(flat(s, t), physical(s, t)) for s in range(SECTIONS) for t in range(8)]
-    return lax.ppermute(array, BOTH, route)
+    return lax.ppermute(array, BOTH, [(a, b) for a, b in route if a != b])
 
 
 def remote(src, dst, send_sem, recv_sem, device):
@@ -49,12 +50,12 @@
 
 def layer_kernel(first, *refs):
     if first:
-        (x_ref, gain_ref, wq_hbm, kv_hbm, wo_hbm, looked_hbm,
-         out_hbm, next_hbm, w_in_hbm, w_out_hbm, *refs) = refs
+        (x_hbm, x_got_hbm, gain_hbm, wq_hbm, wk_hbm, wv_hbm, wo_hbm, looked_hbm,
+         out_hbm, next_hbm, gain_keep, wq_keep, kv_keep, wo_keep, *refs) = refs
     else:
-        (x_ref, gain_ref, w_in_hbm, w_out_hbm, held_hbm, held_out, out_hbm, *refs) = refs
-    (w_in, w_out, normed, q_s, k_s, v_s, ctx, own_part, sib_out, sib_in, ring_out, relay, arrived,
-     out_s, load_sem, kv_sem, ag_send, ag_recv, sib_send, sib_recv, ring_send, ring_recv,
+        (x_hbm, gain_hbm, wq_hbm, kv_hbm, wo_hbm, held_hbm, held_out, out_hbm, *refs) = refs
+    (x_ref, gain_ref, w_q, w_kv, w_out, normed, q_s, k_s, v_s, ctx, own_part, sib_out, sib_in, ring_out, relay, arrived,
+     out_s, load_sem, wo_sem, kv_sem, ag_send, ag_recv, sib_send, sib_recv, ring_send, ring_recv,
      trade_send, trade_recv, out_send, out_recv, *refs) = refs
     if first:
         next_s, e_acc, e_in, e_sem, e_send, e_recv, all_send, all_recv, next_send, next_recv = refs
@@ -124,11 +125,62 @@
             greet((0, t), enters & jnp.logical_not(is_root & (tensor == t)))
         load_looked = pltpu.make_async_copy(looked_hbm, e_acc, e_sem.at[0])
         load_looked.start()
+
+        @pl.when(stays)
+        def _():
+            pltpu.make_async_copy(x_hbm, x_ref, load_sem.at[0]).start()
+
+        @pl.when(moves)
+        def _():
+            pltpu.make_async_copy(x_got_hbm, x_ref, load_sem.at[0]).start()
+
     else:
-        load_in = pltpu.make_async_copy(w_in_hbm, w_in, load_sem.at[0])
-        load_in.start()
-        load_out = pltpu.make_async_copy(w_out_hbm, w_out, load_sem.at[1])
+        load_gain = pltpu.make_async_copy(gain_hbm, gain_ref, load_sem.at[1])
+        load_gain.start()
+        pltpu.make_async_copy(x_hbm, x_ref, load_sem.at[0]).start()
+        load_q = pltpu.make_async_copy(wq_hbm, w_q, load_sem.at[2])
+        load_q.start()
+        load_kv = pltpu.make_async_copy(kv_hbm, w_kv, load_sem.at[3])
+        load_kv.start()
+        load_out = pltpu.make_async_copy(wo_hbm, w_out, load_sem.at[4])
         load_out.start()
+
+    pl.semaphore_wait(barrier, functools.reduce(lambda a, b: a + b, greeted))
+
+    def hand_over(src, dst, slot, sends=trade_send, recvs=trade_recv):
+        @pl.when(stays)
+        def _():
+            pltpu.make_async_copy(src, dst, recvs.at[slot]).start()
+
+        @pl.when(moves)
+        def _():
+            remote(src, dst, sends.at[slot], recvs.at[slot], partner).start()
+
+    def handed(src, dst, slot, sends=trade_send, recvs=trade_recv):
+        remote(src, dst, sends.at[slot], recvs.at[slot], partner).wait_recv()
+
+    def handed_over(src, dst, slot, sends=trade_send, recvs=trade_recv):
+        @pl.when(moves)
+        def _():
+            remote(src, dst, sends.at[slot], recvs.at[slot], partner).wait_send()
+
+    def kv_rows(base, block):
+        return w_kv.at[aligned(base + block * 64, 64), :]
+
+    if first:
+        kv_mine = (kv_rows(0, core), kv_rows(128, core))
+        kv_partner = (kv_rows(0, z_lo), kv_rows(128, z_lo))
+        kv_rest = (kv_rows(0, other), kv_rows(128, other))
+        hand_over(gain_hbm, gain_ref, 0)
+        hand_over(wk_hbm, kv_partner[0], 1)
+        hand_over(wv_hbm, kv_partner[1], 2)
+        hand_over(wq_hbm, w_q, 3)
+        handed(gain_hbm, gain_ref, 0)
+        keep_gain = pltpu.make_async_copy(gain_ref, gain_keep, load_sem.at[1])
+        keep_gain.start()
+    else:
+        load_gain.wait()
+    pltpu.make_async_copy(x_hbm, x_ref, load_sem.at[0]).wait()
 
     def norm_rows(step, carry):
         x = x_ref[aligned(step * 16, 16), :].astype(jnp.float32)
@@ -137,25 +189,6 @@
         return carry
 
     lax.fori_loop(0, ROWS // 16, norm_rows, 0)
-    pl.semaphore_wait(barrier, functools.reduce(lambda a, b: a + b, greeted))
-
-    def hand_over(src, dst, slot, sends=trade_send, recvs=trade_recv):
-        @pl.when(stays)
-        def _():
-            pltpu.make_async_copy(src, dst, recvs.at[slot]).start()
-
-        @pl.when(moves)
-        def _():
-            remote(src, dst, sends.at[slot], recvs.at[slot], partner).start()
-
-    def handed(src, dst, slot, sends=trade_send, recvs=trade_recv):
-        remote(src, dst, sends.at[slot], recvs.at[slot], partner).wait_recv()
-
-    def handed_over(src, dst, slot, sends=trade_send, recvs=trade_recv):
-        @pl.when(moves)
-        def _():
-            remote(src, dst, sends.at[slot], recvs.at[slot], partner).wait_send()
-
     sends = []
 
     def piece(chip, side, half):
@@ -200,30 +233,34 @@
         rows = aligned(chip * PAIR, PAIR)
 
         def two_heads(n, carry):
-            res = jnp.dot(normed[chip], w_in[:, aligned(n * 256, 256)], preferred_element_type=jnp.float32)
+            res = jnp.dot(normed[chip], w_q[:, aligned(n * 256, 256)], preferred_element_type=jnp.float32)
             q_s[2 * n, rows, :] = res[:, :128].astype(jnp.bfloat16)
             q_s[2 * n + 1, rows, :] = res[:, 128:].astype(jnp.bfloat16)
             return carry
 
         lax.fori_loop(0, 2, two_heads, 0)
-        res = jnp.dot(normed[chip], w_in[:, 512:768], preferred_element_type=jnp.float32)
-        k_s[rows, :] = jnp.concatenate([res[:, 0:64], res[:, 128:192]], axis=1).astype(jnp.bfloat16)
-        v_s[rows, :] = jnp.concatenate([res[:, 64:128], res[:, 192:256]], axis=1).astype(jnp.bfloat16)
+        res = lax.dot_general(
+            normed[chip], w_kv[...], (((1,), (1,)), ((), ())), preferred_element_type=jnp.float32
+        )
+        k_s[rows, :] = res[:, :128].astype(jnp.bfloat16)
+        v_s[rows, :] = res[:, 128:].astype(jnp.bfloat16)
 
     def out_cols(n):
         return aligned(n * PART, PART)
 
     if first:
-        kv_own = w_in.at[:, aligned(512 + core * 128, 128)]
-        kv_partner = w_in.at[:, aligned(512 + z_lo * 128, 128)]
-        kv_rest = w_in.at[:, aligned(512 + other * 128, 128)]
-        wq_slot = w_in.at[:, pl.ds(0, 512)]
-
         def wo_part(n):
-            return (wo_hbm.at[:, out_cols(n)], w_out.at[:, out_cols(n)], 2 + n)
-
-        hand_over(kv_hbm, kv_partner, 0)
-        hand_over(wq_hbm, wq_slot, 1)
+            return (wo_hbm.at[:, out_cols(n)], w_out.at[:, out_cols(n)], 4 + n)
+
+        def keep_part(n):
+            return pltpu.make_async_copy(w_out.at[:, out_cols(n)], wo_keep.at[:, out_cols(n)], wo_sem.at[n])
+
+        def advance(n):
+            handed_over(*wo_part(n))
+
+            @pl.when(n < PARTS - AHEAD)
+            def _():
+                hand_over(*wo_part(n + AHEAD))
 
         def tree(slot, src, device):
             return remote(src, e_in.at[slot], e_send.at[slot], e_recv.at[slot], device)
@@ -272,20 +309,24 @@
         def _():
             tree(3, e_acc, (pipe - 8, tensor)).start()
 
-        handed(kv_hbm, kv_own, 0)
-        share = remote(kv_own, kv_own, kv_sem.at[0], kv_sem.at[1], sibling)
-        share.start()
-        handed(wq_hbm, wq_slot, 1)
-        handed_over(kv_hbm, kv_partner, 0)
-        handed_over(wq_hbm, wq_slot, 1)
-        for n in range(2):
+        shares = []
+        for i in range(2):
+            handed((wk_hbm, wv_hbm)[i], kv_mine[i], 1 + i)
+            shares.append(remote(kv_mine[i], kv_mine[i], kv_sem.at[i], kv_sem.at[2 + i], sibling))
+            shares[i].start()
+        handed_over(wq_hbm, w_q, 3)
+        for n in range(AHEAD):
             hand_over(*wo_part(n))
-        remote(kv_rest, kv_rest, kv_sem.at[0], kv_sem.at[1], sibling).wait_recv()
-        keep_in = pltpu.make_async_copy(w_in, w_in_hbm, load_sem.at[0])
-        keep_in.start()
+        handed(wq_hbm, w_q, 3)
+        for i in range(2):
+            remote(kv_rest[i], kv_rest[i], kv_sem.at[i], kv_sem.at[2 + i], sibling).wait_recv()
+        keep_q = pltpu.make_async_copy(w_q, wq_keep, load_sem.at[2])
+        keep_q.start()
+        keep_kv = pltpu.make_async_copy(w_kv, kv_keep, load_sem.at[3])
+        keep_kv.start()
         for chip in range(RING):
             for side in range(2):
-                @pl.when((side != core) | False)
+                @pl.when(core != side)
                 def _(chip=chip, side=side):
                     wait_piece(chip, side, 0)
                     wait_piece(chip, side, 1)
@@ -300,7 +341,8 @@
         hand_over(held_src, held_out, 0)
         wait_piece(y, other, 0)
         wait_piece(y, other, 1)
-        load_in.wait()
+        load_q.wait()
+        load_kv.wait()
         project(y)
         forward_near()
         for chip in (y_down, y_up):
@@ -330,6 +372,8 @@
             weights = (exps * (1.0 / jnp.sum(exps, axis=1, keepdims=True))).astype(jnp.bfloat16)
             mixed = jnp.dot(weights, v_s[:keys, :], preferred_element_type=jnp.float32)
             ctx[i, :, cols] = mixed.astype(jnp.bfloat16)
+        if first:
+            advance(h)
         return carry
 
     lax.fori_loop(0, HEADS_DEV, head, 0)
@@ -388,11 +432,11 @@
     def project_part(n):
         if first:
             handed(*wo_part(n))
-            handed_over(*wo_part(n))
-
-            @pl.when(n < PARTS - 2)
+            keep_part(n).start()
+
+            @pl.when(n >= HEADS_DEV)
             def _():
-                hand_over(*wo_part(n + 2))
+                advance(n)
 
         def slot_step(slot, carry):
             chip = lax.rem(y + 6 - slot, RING)
@@ -479,11 +523,14 @@
     lax.fori_loop(0, PARTS + 3, pipeline, 0)
 
     if first:
-        keep_out = pltpu.make_async_copy(w_out, w_out_hbm, load_sem.at[1])
-        keep_out.start()
-        share.wait_send()
-        keep_in.wait()
-        keep_out.wait()
+        for copy in shares:
+            copy.wait_send()
+        handed_over(gain_hbm, gain_ref, 0)
+        handed_over(wk_hbm, kv_partner[0], 1)
+        handed_over(wv_hbm, kv_partner[1], 2)
+        keep_gain.wait()
+        keep_q.wait()
+        keep_kv.wait()
 
         @pl.when(core == 1)
         def _():
@@ -537,6 +584,7 @@
                 next_copy(n, after).wait_recv()
 
             pltpu.make_async_copy(out_s.at[n], out_hbm.at[:, out_cols(n)], out_recv.at[n]).wait()
+            keep_part(n).wait()
         else:
             handed(*out_part(n), out_send, out_recv)
             handed_over(*out_part(n), out_send, out_recv)
@@ -548,20 +596,24 @@
 def layer(first, *operands):
     bf16, f32 = jnp.bfloat16, jnp.float32
     dma = pltpu.SemaphoreType.DMA
-    vmem = pl.BlockSpec(memory_space=pltpu.VMEM)
     hbm = pl.BlockSpec(memory_space=pl.ANY)
     block = jax.ShapeDtypeStruct((ROWS, WIDTH), f32)
     if first:
         out_shape = (
             block,
             jax.ShapeDtypeStruct((ROWS, WIDTH), bf16),
-            jax.ShapeDtypeStruct((WIDTH, 768), bf16),
+            jax.ShapeDtypeStruct((1, WIDTH), f32),
+            jax.ShapeDtypeStruct((WIDTH, 512), bf16),
+            jax.ShapeDtypeStruct((256, WIDTH), bf16),
             jax.ShapeDtypeStruct((512, WIDTH), bf16),
         )
     else:
         out_shape = (block, block)
     scratch = [
-        pltpu.VMEM((WIDTH, 768), bf16),
+        pltpu.VMEM((ROWS, WIDTH), bf16),
+        pltpu.VMEM((1, WIDTH), f32),
+        pltpu.VMEM((WIDTH, 512), bf16),
+        pltpu.VMEM((256, WIDTH), bf16),
         pltpu.VMEM((512, WIDTH), bf16),
         pltpu.VMEM((RING, PAIR, WIDTH), bf16),
         pltpu.VMEM((HEADS_DEV, TOKENS, HEAD_DIM), bf16),
@@ -575,9 +627,9 @@
         pltpu.VMEM((PARTS, 2, HALF, PART), bf16),
         pltpu.VMEM((PARTS, 2, ROWS, PART), bf16),
         pltpu.VMEM((PARTS, ROWS, PART), f32),
-        dma((2,)), dma((2,)), dma((14,)), dma((RING, 2, 2)),
+        dma((5,)), dma((PARTS,)), dma((4,)), dma((14,)), dma((RING, 2, 2)),
         dma((PARTS,)), dma((PARTS,)), dma((PARTS, 6)), dma((PARTS, 6)),
-        dma((2 + PARTS,)), dma((2 + PARTS,)), dma((PARTS,)), dma((PARTS,)),
+        dma((4 + PARTS,)), dma((4 + PARTS,)), dma((PARTS,)), dma((PARTS,)),
     ]
     if first:
         scratch += [
@@ -589,7 +641,7 @@
     return pl.pallas_call(
         functools.partial(layer_kernel, first),
         out_shape=out_shape,
-        in_specs=[vmem, vmem] + [hbm] * (len(operands) - 2),
+        in_specs=[hbm] * len(operands),
         out_specs=tuple(hbm for _ in out_shape),
         scratch_shapes=scratch,
         compiler_params=pltpu.CompilerParams(
@@ -616,13 +668,11 @@
     inside = (local_index >= 0) & (local_index < vocab_dev)
     looked = jnp.take(lookup_table_matrix, jnp.clip(local_index, 0, vocab_dev - 1), axis=0)
     looked = jnp.where(inside[:, None], looked, jnp.zeros_like(looked))
-    kv = jnp.concatenate([key_projector[0], value_projector[0]], axis=1)
-    gain = traded(scale_factors)
-    first_in = traded(pending_batches)
-    first_held, second_in, w_in, w_out = layer(
-        True, first_in, gain, query_projector[0], kv, result_projector[0], looked
+    first_held, second_in, *weights = layer(
+        True, pending_batches, from_partner(pending_batches), scale_factors, query_projector[0],
+        key_projector[0].T, value_projector[0].T, result_projector[0], looked,
     )
-    return layer(False, second_in, gain, w_in, w_out, first_held)
+    return layer(False, second_in, *weights, first_held)
 
 
 def solution(mesh):

time: 287 us -> 272 us (0.948)
  the two profiles are of different devices: /device:TPU:1 before, /device:TPU:69 now
where the time goes in v3:
time: 272 us
  Pallas kernels  249 us (92%)
  local copies, waits for them, and re-layouts  14 us (5%)
  starting transfers between devices  3.81 us (1%)
    pallas_call x2, Pallas kernels, layer(): pl.pallas_call(functools.partial(layer_kernel, first), out_shape=out_shap...  249 us
    gather x1, local copies, waits for them, and re-layouts, body(): jnp.take(lookup_table_matrix, jnp.clip(local_index, 0, vocab_dev - 1), ax...  8.46 us
    unnamed x8, local copies, waits for them, and re-layouts  5.56 us
  transfers between devices with their start and end apart: 1, of which 1 were waited for; matrix products, arithmetic and copies ran while one was open for 4% of the time, Pallas kernels for 0%

profile of v3, /device:TPU:69, one launch (start us, length us, event | category | flops | bytes accessed | tf_op | source)
XLA Modules:
  0.0 272.0 jit_solution(15728850302429302480)
XLA Ops:
  0.6 3.8 %collective-permute-start = (bf16[128,4096]{1,0:T(8,128)(2,1)}, bf16[128,4096]{1,0:T(8,128)(2,1)S(1)}, u32[]{:S(2)}, u32[]{:S(2)}) collective-permute-start(bf16[128,4096]{1,0:T(8,128)(2,1)} %refs_0_.1), channel_id=1, source_target_pairs={{1,8},{3,10},{5,12},{7,14},{8,1},{10,3},{12,5},{14,7},{17,24},{19,... | collective-permute-start | bytes 3145736 | tf_op jit(solution)/shard_map/ppermute | solution.py:37
  4.5 0.7 fusion
  5.2 0.0 copy-start.1
  5.2 8.5 %gather_fusion = bf16[1024,512]{1,0:T(8,128)(2,1)S(1)} fusion(bf16[8192,512]{1,0:T(8,128)(2,1)} %param.9, s32[1024]{0:T(1024)S(1)} %fusion), kind=kCustom, calls=%fused_computation | custom fusion | bytes 2101248 | tf_op jit(solution)/shard_map/jit(_take)/gather | solution.py:669
  13.6 0.0 copy-done.1
  13.7 1.6 select_select_fusion.refs_7_
  15.3 1.9 collective-permute-done.refs_1_
  17.1 0.0 copy-start.2
  17.1 1.0 copy-done.2
  18.1 147.8 %first_layer.1 = (f32[128,4096]{1,0:T(8,128)}, bf16[128,4096]{1,0:T(8,128)(2,1)}, f32[1,4096]{1,0:T(1,128)}, bf16[4096,512]{1,0:T(8,128)(2,1)}, bf16[256,4096]{1,0:T(8,128)(2,1)}, /*index=5*/bf16[512,4096]{1,0:T(8,128)(2,1)}) custom-call(bf16[128,4096]{1,0:T(8,128)(2,1)} %refs_0_.1, bf16[128,4096]{1,0:T(8,128)(2,1)} %copy-done.2, f32[1,4096]{1,0:T(1,128)} %refs_2_.1, ...), custom_call_target="tpu_custom_call" | custom-call | flops 12000000000 | bytes 16777216 | tf_op jit(solution)/shard_map/first_layer/pallas_call | solution.py:641
  165.9 101.5 %second_layer.1 = (f32[128,4096]{1,0:T(8,128)}, f32[128,4096]{1,0:T(8,128)}) custom-call(bf16[128,4096]{1,0:T(8,128)(2,1)} %get-tuple-element.8.refs_0_, f32[1,4096]{1,0:T(1,128)} %get-tuple-element.9.refs_1_, bf16[4096,512]{1,0:T(8,128)(2,1)} %get-tuple-element.10.refs_2_, bf16[256,4096]{1,0:T(8,128)(2,1)} %get-tuple-element.11.refs_3_, ...), custom_call_target="tpu_custom_call" | custom-call | flops 12000000000 | bytes 16777216 | tf_op jit(solution)/shard_map/second_layer/pallas_call | solution.py:641
  267.4 0.0 copy-start
  267.4 3.3 %copy.12 = f32[128,4096]{1,0:T(8,128)} copy(f32[128,4096]{1,0:T(8,128)} %get-tuple-element.18) | data formatting | bytes 4194304
  270.7 0.0 copy-done
  270.7 1.3 copy.13
  (1 shorter events, 0.0 us)
Async XLA Ops:
  0.6 16.5 %collective-permute-start = (bf16[128,4096]{1,0:T(8,128)(2,1)}, bf16[128,4096]{1,0:T(8,128)(2,1)S(1)}, u32[]{:S(2)}, u32[]{:S(2)}) collective-permute-start(bf16[128,4096]{1,0:T(8,128)(2,1)} %refs_0_.1), channel_id=1, source_target_pairs={{1,8},{3,10},{5,12},{7,14},{8,1},{10,3},{12,5},{14,7},{17,24},{19,... | collective-permute-start | bytes 3145736 | tf_op jit(solution)/shard_map/ppermute | solution.py:37
  5.2 8.5 %copy-start.1 = (s32[1024]{0:T(1024)S(1)}, s32[1024]{0:T(1024)}, u32[]{:S(2)}) copy-start(s32[1024]{0:T(1024)} %param.8) | copy-start | bytes 12292
  17.1 1.0 copy-start.2
  267.4 3.3 %copy-start = (f32[128,4096]{1,0:T(8,128)S(1)}, f32[128,4096]{1,0:T(8,128)}, u32[]{:S(2)}) copy-start(f32[128,4096]{1,0:T(8,128)} %get-tuple-element.19) | copy-start | bytes 6291460

commit v4 on v3

--- a/solution.py
+++ b/solution.py
@@ -21,7 +21,6 @@
 HALF = ROWS // 2
 PARTS = 8
 PART = WIDTH // PARTS
-AHEAD = 3
 
 
 def flat(pipe, tensor):
@@ -255,12 +254,8 @@
         def keep_part(n):
             return pltpu.make_async_copy(w_out.at[:, out_cols(n)], wo_keep.at[:, out_cols(n)], wo_sem.at[n])
 
-        def advance(n):
-            handed_over(*wo_part(n))
-
-            @pl.when(n < PARTS - AHEAD)
-            def _():
-                hand_over(*wo_part(n + AHEAD))
+        for n in range(PARTS):
+            hand_over(*wo_part(n))
 
         def tree(slot, src, device):
             return remote(src, e_in.at[slot], e_send.at[slot], e_recv.at[slot], device)
@@ -314,9 +309,6 @@
             handed((wk_hbm, wv_hbm)[i], kv_mine[i], 1 + i)
             shares.append(remote(kv_mine[i], kv_mine[i], kv_sem.at[i], kv_sem.at[2 + i], sibling))
             shares[i].start()
-        handed_over(wq_hbm, w_q, 3)
-        for n in range(AHEAD):
-            hand_over(*wo_part(n))
         handed(wq_hbm, w_q, 3)
         for i in range(2):
             remote(kv_rest[i], kv_rest[i], kv_sem.at[i], kv_sem.at[2 + i], sibling).wait_recv()
@@ -372,8 +364,6 @@
             weights = (exps * (1.0 / jnp.sum(exps, axis=1, keepdims=True))).astype(jnp.bfloat16)
             mixed = jnp.dot(weights, v_s[:keys, :], preferred_element_type=jnp.float32)
             ctx[i, :, cols] = mixed.astype(jnp.bfloat16)
-        if first:
-            advance(h)
         return carry
 
     lax.fori_loop(0, HEADS_DEV, head, 0)
@@ -433,10 +423,6 @@
         if first:
             handed(*wo_part(n))
             keep_part(n).start()
-
-            @pl.when(n >= HEADS_DEV)
-            def _():
-                advance(n)
 
         def slot_step(slot, carry):
             chip = lax.rem(y + 6 - slot, RING)
@@ -528,6 +514,7 @@
         handed_over(gain_hbm, gain_ref, 0)
         handed_over(wk_hbm, kv_partner[0], 1)
         handed_over(wv_hbm, kv_partner[1], 2)
+        handed_over(wq_hbm, w_q, 3)
         keep_gain.wait()
         keep_q.wait()
         keep_kv.wait()
@@ -585,6 +572,7 @@
 
             pltpu.make_async_copy(out_s.at[n], out_hbm.at[:, out_cols(n)], out_recv.at[n]).wait()
             keep_part(n).wait()
+            handed_over(*wo_part(n))
         else:
             handed(*out_part(n), out_send, out_recv)
             handed_over(*out_part(n), out_send, out_recv)

time: 272 us -> 296 us (1.088)
  the two profiles are of different devices: /device:TPU:69 before, /device:TPU:1 now
where the time goes in v4:
time: 296 us; the launch traced here: 295 us
  Pallas kernels  272 us (92%)
  local copies, waits for them, and re-layouts  14 us (5%)
  starting transfers between devices  4.94 us (2%)
    pallas_call x2, Pallas kernels, layer(): pl.pallas_call(functools.partial(layer_kernel, first), out_shape=out_shap...  272 us
    gather x1, local copies, waits for them, and re-layouts, body(): jnp.take(lookup_table_matrix, jnp.clip(local_index, 0, vocab_dev - 1), ax...  8.46 us
  transfers between devices with their start and end apart: 1, of which 1 were waited for; matrix products, arithmetic and copies ran while one was open for 4% of the time, Pallas kernels for 0%

profile of v4, /device:TPU:1, one launch (start us, length us, event | category | flops | bytes accessed | tf_op | source)
XLA Modules:
  0.0 295.4 jit_solution(13394565583401242298)
XLA Ops:
  0.6 4.9 %collective-permute-start = (bf16[128,4096]{1,0:T(8,128)(2,1)}, bf16[128,4096]{1,0:T(8,128)(2,1)S(1)}, u32[]{:S(2)}, u32[]{:S(2)}) collective-permute-start(bf16[128,4096]{1,0:T(8,128)(2,1)} %refs_0_.1), channel_id=1, source_target_pairs={{1,8},{3,10},{5,12},{7,14},{8,1},{10,3},{12,5},{14,7},{17,24},{19,... | collective-permute-start | bytes 3145736 | tf_op jit(solution)/shard_map/ppermute | solution.py:36
  5.6 0.7 fusion
  6.3 0.0 copy-start.1
  6.3 8.5 %gather_fusion = bf16[1024,512]{1,0:T(8,128)(2,1)S(1)} fusion(bf16[8192,512]{1,0:T(8,128)(2,1)} %param.9, s32[1024]{0:T(1024)S(1)} %fusion), kind=kCustom, calls=%fused_computation | custom fusion | bytes 2101248 | tf_op jit(solution)/shard_map/jit(_take)/gather | solution.py:657
  14.7 0.0 copy-done.1
  14.8 1.6 select_select_fusion.refs_7_
  16.4 1.9 collective-permute-done.refs_1_
  18.3 0.0 copy-start.2
  18.3 1.0 copy-done.2
  19.2 137.4 %first_layer.1 = (f32[128,4096]{1,0:T(8,128)}, bf16[128,4096]{1,0:T(8,128)(2,1)}, f32[1,4096]{1,0:T(1,128)}, bf16[4096,512]{1,0:T(8,128)(2,1)}, bf16[256,4096]{1,0:T(8,128)(2,1)}, /*index=5*/bf16[512,4096]{1,0:T(8,128)(2,1)}) custom-call(bf16[128,4096]{1,0:T(8,128)(2,1)} %refs_0_.1, bf16[128,4096]{1,0:T(8,128)(2,1)} %copy-done.2, f32[1,4096]{1,0:T(1,128)} %refs_2_.1, ...), custom_call_target="tpu_custom_call" | custom-call | flops 12000000000 | bytes 16777216 | tf_op jit(solution)/shard_map/first_layer/pallas_call | solution.py:629
  156.6 134.2 %second_layer.1 = (f32[128,4096]{1,0:T(8,128)}, f32[128,4096]{1,0:T(8,128)}) custom-call(bf16[128,4096]{1,0:T(8,128)(2,1)} %get-tuple-element.8.refs_0_, f32[1,4096]{1,0:T(1,128)} %get-tuple-element.9.refs_1_, bf16[4096,512]{1,0:T(8,128)(2,1)} %get-tuple-element.10.refs_2_, bf16[256,4096]{1,0:T(8,128)(2,1)} %get-tuple-element.11.refs_3_, ...), custom_call_target="tpu_custom_call" | custom-call | flops 12000000000 | bytes 16777216 | tf_op jit(solution)/shard_map/second_layer/pallas_call | solution.py:629
  290.8 0.0 copy-start
  290.8 3.3 %copy.12 = f32[128,4096]{1,0:T(8,128)} copy(f32[128,4096]{1,0:T(8,128)} %get-tuple-element.18) | data formatting | bytes 4194304
  294.1 0.0 copy-done
  294.1 1.3 copy.13
  (1 shorter events, 0.0 us)
Async XLA Ops:
  0.6 17.6 %collective-permute-start = (bf16[128,4096]{1,0:T(8,128)(2,1)}, bf16[128,4096]{1,0:T(8,128)(2,1)S(1)}, u32[]{:S(2)}, u32[]{:S(2)}) collective-permute-start(bf16[128,4096]{1,0:T(8,128)(2,1)} %refs_0_.1), channel_id=1, source_target_pairs={{1,8},{3,10},{5,12},{7,14},{8,1},{10,3},{12,5},{14,7},{17,24},{19,... | collective-permute-start | bytes 3145736 | tf_op jit(solution)/shard_map/ppermute | solution.py:36
  6.3 8.5 %copy-start.1 = (s32[1024]{0:T(1024)S(1)}, s32[1024]{0:T(1024)}, u32[]{:S(2)}) copy-start(s32[1024]{0:T(1024)} %param.8) | copy-start | bytes 12292
  18.3 1.0 copy-start.2
  290.8 3.3 %copy-start = (f32[128,4096]{1,0:T(8,128)S(1)}, f32[128,4096]{1,0:T(8,128)}, u32[]{:S(2)}) copy-start(f32[128,4096]{1,0:T(8,128)} %get-tuple-element.19) | copy-start | bytes 6291460

commit v5 on v0

v5 whole, which is shorter than its diff:
```python
import functools

import jax
import jax.numpy as jnp
from jax import lax
from jax.experimental import pallas as pl
from jax.experimental.pallas import tpu as pltpu
from jax.sharding import PartitionSpec as P

HEAD_DIM = 128
MESH = pl.DeviceIdType.MESH
SECTIONS = 16
RING = 4
TOKENS = 1024
ROWS = 128
WIDTH = 4096
COLS = 512
HEADS_DEV = 4
PAIR = 2 * ROWS
HALF = ROWS // 2
PARTS = 8
PART = WIDTH // PARTS
HELD = 4
VOCAB_DEV = 8192
CHUNK = 1024
CHUNKS = VOCAB_DEV // CHUNK
QUARTER = TOKENS // 4


def remote(src, dst, send_sem, recv_sem, device):
    return pltpu.make_async_remote_copy(
        src_ref=src, dst_ref=dst, send_sem=send_sem, recv_sem=recv_sem,
        device_id=device, device_id_type=MESH,
    )


def aligned(start, size):
    return pl.ds(pl.multiple_of(start, size), size)


def relay_kernel(
    ids_ref, table_hbm, x_hbm, gain_hbm, wq_hbm, wk_hbm, wv_hbm, wo_hbm,
    first_out, second_out,
    x_s, gain_s, w_q, w_kv, w_out, normed, q_s, k_s, v_s, ctx, own_part, sib_out, sib_in, ring_out, relay,
    arrived, out_s, next_s, table_s, e_acc, e_in, e_side, e_sum, e_far,
    table_sem, kv_sem, ag_send, ag_recv, sib_send, sib_recv, ring_send, ring_recv,
    trade_send, trade_recv, out_send, out_recv, next_send, next_recv,
    core_sem, side_send, side_recv, far_sem, all_send, all_recv,
):
    pipe = lax.axis_index("pipe")
    tensor = lax.axis_index("tensor")
    core = lax.rem(pipe, 2)
    x_pos = lax.rem(lax.div(pipe, 2), 4)
    z_hi = lax.div(pipe, 8)
    y = lax.div(tensor, 2)
    z_lo = lax.rem(tensor, 2)
    y_up = lax.rem(y + 1, RING)
    y_far = lax.rem(y + 2, RING)
    y_down = lax.rem(y + 3, RING)
    other = 1 - core
    section = pipe - core + z_lo
    sibling = (pipe + 1 - 2 * core, tensor)
    up = (pipe, 2 * y_up + z_lo)
    down = (pipe, 2 * y_down + z_lo)
    stays = core == z_lo
    moves = core != z_lo
    partner = (pipe - core + z_lo, tensor - z_lo + core)
    has_next = section < SECTIONS - 1
    has_prev = section > 0
    after = (pipe + 2 * z_lo, tensor + 1 - 2 * z_lo)
    before = (pipe - 2 * (1 - z_lo), tensor + 1 - 2 * z_lo)
    lead = core == 0
    lead_near = lead & (z_hi == 0)
    lead_far = lead & (z_hi == 1)
    enters = section == 0

    def side(distance):
        return (z_hi * 8 + 2 * lax.rem(x_pos + distance, 4) + core, tensor)

    def owner(row_block):
        return (row_block, 2 * x_pos)

    def is_owner(row_block):
        return (pipe == row_block) & (tensor == 2 * x_pos)

    barrier = pltpu.get_barrier_semaphore()
    greeted = []

    def greet(device, condition=None):
        def signal():
            pl.semaphore_signal(barrier, inc=1, device_id=device, device_id_type=MESH)

        if condition is None:
            signal()
            greeted.append(1)
        else:
            pl.when(condition)(signal)
            greeted.append(jnp.where(condition, 1, 0))

    greet(sibling)
    greet(up)
    greet(down)
    greet(partner, moves)
    greet(after, has_next)
    greet(before, has_prev)
    for distance in (1, 2, 3):
        greet(side(distance), lead)
    greet((pipe + 8, tensor), lead_near)
    greet((pipe - 8, tensor), lead_far)
    for row_block in range(2):
        greet(owner(row_block), lead_near & jnp.logical_not(is_owner(row_block)))
    for t in range(8):
        greet((2 * y, t), enters & jnp.logical_not((pipe == 2 * y) & (tensor == t)))

    def table_copy(c):
        slot = lax.rem(c, 2)
        return pltpu.make_async_copy(
            table_hbm.at[aligned(c * CHUNK, CHUNK), :], table_s.at[slot], table_sem.at[slot]
        )

    table_copy(0).start()
    table_copy(1).start()
    e_acc[...] = jnp.zeros_like(e_acc)
    pl.semaphore_wait(barrier, functools.reduce(lambda a, b: a + b, greeted))

    def hand_over(src, dst, sends, recvs):
        @pl.when(stays)
        def _():
            pltpu.make_async_copy(src, dst, recvs).start()

        @pl.when(moves)
        def _():
            remote(src, dst, sends, recvs, partner).start()

    def handed(src, dst, sends, recvs):
        remote(src, dst, sends, recvs, partner).wait_recv()

    def handed_over(src, dst, sends, recvs):
        @pl.when(moves)
        def _():
            remote(src, dst, sends, recvs, partner).wait_send()

    def out_cols(n):
        return aligned(n * PART, PART)

    def kv_rows(base, block):
        return w_kv.at[aligned(base + block * 64, 64), :]

    def traded(src, dst, slot):
        return (src, dst, trade_send.at[slot], trade_recv.at[slot])

    kv_mine = (kv_rows(0, core), kv_rows(128, core))
    kv_rest = (kv_rows(0, other), kv_rows(128, other))
    gain_trade = traded(gain_hbm, gain_s, 0)
    x_trade = traded(x_hbm, x_s.at[0], 1)
    kv_trade = (traded(wk_hbm, kv_rows(0, z_lo), 2), traded(wv_hbm, kv_rows(128, z_lo), 3))
    wq_trade = traded(wq_hbm, w_q, 4)

    def wo_trade(n):
        return traded(wo_hbm.at[:, out_cols(n)], w_out.at[:, out_cols(n)], 5 + n)

    for trade in (gain_trade, x_trade, *kv_trade, wq_trade):
        hand_over(*trade)

    def look_up(c, carry):
        table_copy(c).wait()
        start = pipe * VOCAB_DEV + c * CHUNK

        def tile(step, inner):
            rows = aligned(step * 256, 256)
            row_ids = ids_ref[rows, :] - start
            hit = row_ids == lax.broadcasted_iota(jnp.int32, (256, CHUNK), 1)
            ones = jnp.where(hit, 1.0, 0.0).astype(jnp.bfloat16)
            found = jnp.dot(ones, table_s[lax.rem(c, 2)], preferred_element_type=jnp.float32)
            e_acc[rows, :] = e_acc[rows, :] + found.astype(jnp.bfloat16)
            return inner

        lax.fori_loop(0, TOKENS // 256, tile, 0)

        @pl.when(c < CHUNKS - 2)
        def _():
            table_copy(c + 2).start()

        return carry

    def add_rows(into, count, term):
        def rows_step(step, carry):
            rows = aligned(step * 64, 64)
            into[rows, :] = into[rows, :] + term[rows, :]
            return carry

        lax.fori_loop(0, count // 64, rows_step, 0)

    core_copy = remote(e_acc, e_in, core_sem.at[0], core_sem.at[1], sibling)

    def side_copy(distance):
        quarter = aligned(lax.rem(x_pos + distance, 4) * QUARTER, QUARTER)
        return remote(
            e_acc.at[quarter, :], e_side.at[distance - 1],
            side_send.at[distance - 1], side_recv.at[distance - 1], side(distance),
        )

    far_copy = remote(e_sum, e_far, far_sem.at[0], far_sem.at[1], (pipe - 8, tensor))

    def entry_copy(row_block, column):
        return (
            e_sum.at[pl.ds(row_block * ROWS, ROWS), :],
            x_s.at[1, :, aligned(column * COLS, COLS)],
        )

    def next_copy(n):
        return remote(next_s.at[n], x_s.at[1, :, out_cols(n)], next_send.at[n], next_recv.at[n], after)

    low, high = pl.ds(0, HALF), pl.ds(HALF, HALF)
    ring_plan = (
        (0, low, "relay", 0, up),
        (0, high, "relay", 1, down),
        (1, high, "arrived", 0, up),
        (2, low, "arrived", 1, down),
        (1, low, "arrived", 0, up),
        (2, high, "arrived", 1, down),
    )

    def layer(l):
        first = l == 0

        def norm_rows(step, carry):
            x = x_s[l, aligned(step * 16, 16), :].astype(jnp.float32)
            factor = lax.rsqrt(jnp.mean(x * x, axis=1, keepdims=True) + 1e-05)
            normed[y, aligned(core * ROWS + step * 16, 16), :] = (x * factor * gain_s[...]).astype(jnp.bfloat16)
            return carry

        lax.fori_loop(0, ROWS // 16, norm_rows, 0)

        sends = []

        def piece(chip, owner_core, half):
            return normed.at[chip, aligned(owner_core * ROWS + half * HALF, HALF), :]

        def gather(chip, owner_core, half, device):
            part = piece(chip, owner_core, half)
            copy = remote(part, part, ag_send.at[l, len(sends)], ag_recv.at[l, chip, owner_core, half], device)
            copy.start()
            sends.append(copy)

        def wait_piece(chip, owner_core, half):
            part = piece(chip, owner_core, half)
            remote(part, part, ag_send.at[l, 0], ag_recv.at[l, chip, owner_core, half], sibling).wait_recv()

        gather(y, core, 0, up)
        gather(y, core, 1, down)
        gather(y, core, 0, sibling)
        gather(y, core, 1, sibling)
        gather(y, core, 1, up)
        gather(y, core, 0, down)

        def forward_near():
            wait_piece(y_down, core, 0)
            gather(y_down, core, 0, up)
            gather(y_down, core, 0, sibling)
            wait_piece(y_up, core, 1)
            gather(y_up, core, 1, down)
            gather(y_up, core, 1, sibling)
            wait_piece(y_down, core, 1)
            gather(y_down, core, 1, sibling)
            wait_piece(y_up, core, 0)
            gather(y_up, core, 0, sibling)

        def forward_far():
            wait_piece(y_far, core, 0)
            gather(y_far, core, 0, sibling)
            wait_piece(y_far, core, 1)
            gather(y_far, core, 1, sibling)

        def project(chip):
            rows = aligned(chip * PAIR, PAIR)

            def two_heads(n, carry):
                res = jnp.dot(normed[chip], w_q[:, aligned(n * 256, 256)], preferred_element_type=jnp.float32)
                q_s[2 * n, rows, :] = res[:, :128].astype(jnp.bfloat16)
                q_s[2 * n + 1, rows, :] = res[:, 128:].astype(jnp.bfloat16)
                return carry

            lax.fori_loop(0, 2, two_heads, 0)
            res = lax.dot_general(
                normed[chip], w_kv[...], (((1,), (1,)), ((), ())), preferred_element_type=jnp.float32
            )
            k_s[rows, :] = res[:, :128].astype(jnp.bfloat16)
            v_s[rows, :] = res[:, 128:].astype(jnp.bfloat16)

        if first:
            lax.fori_loop(CHUNKS // 2, CHUNKS, look_up, 0)

            @pl.when(core == 1)
            def _():
                core_copy.start()

            forward_near()

            @pl.when(lead)
            def _():
                core_copy.wait_recv()
                add_rows(e_acc, TOKENS, e_in)
                for distance in (1, 2, 3):
                    side_copy(distance).start()

            forward_far()

            @pl.when(lead)
            def _():
                e_sum[...] = e_acc[aligned(x_pos * QUARTER, QUARTER), :]
                for distance in (1, 2, 3):
                    side_copy(distance).wait_recv()
                    add_rows(e_sum, QUARTER, e_side.at[distance - 1])

            @pl.when(lead_far)
            def _():
                far_copy.start()

            for n in range(PARTS):
                hand_over(*wo_trade(n))
            shares = []
            for i in range(2):
                handed(*kv_trade[i][:1], kv_mine[i], *kv_trade[i][2:])
                shares.append(remote(kv_mine[i], kv_mine[i], kv_sem.at[i], kv_sem.at[2 + i], sibling))
                shares[i].start()
            handed(*wq_trade)
            for i in range(2):
                remote(kv_rest[i], kv_rest[i], kv_sem.at[i], kv_sem.at[2 + i], sibling).wait_recv()
            for chip in range(RING):
                for owner_core in range(2):
                    @pl.when(core != owner_core)
                    def _(chip=chip, owner_core=owner_core):
                        wait_piece(chip, owner_core, 0)
                        wait_piece(chip, owner_core, 1)

            def project_step(chip, carry):
                project(chip)
                return carry

            lax.fori_loop(0, RING, project_step, 0)
        else:
            for n in range(PARTS):
                hand_over(*returned(0, n))
            wait_piece(y, other, 0)
            wait_piece(y, other, 1)
            project(y)
            forward_near()
            for chip in (y_down, y_up):
                wait_piece(chip, other, 0)
                wait_piece(chip, other, 1)
                project(chip)
            forward_far()
            wait_piece(y_far, other, 0)
            wait_piece(y_far, other, 1)
            project(y_far)

        scale = HEAD_DIM ** (-0.5)
        seen = lax.broadcasted_iota(jnp.int32, (PAIR, PAIR), 0) >= lax.broadcasted_iota(jnp.int32, (PAIR, PAIR), 1)

        def against(query, keys):
            return lax.dot_general(query, keys, (((1,), (1,)), ((), ())), preferred_element_type=jnp.float32)

        def head(h, carry):
            cols = aligned(h * HEAD_DIM, HEAD_DIM)
            for i in range(RING):
                before_rows, rows = PAIR * i, slice(PAIR * i, PAIR * (i + 1))
                query = q_s[h, rows, :]
                near = jnp.where(seen, against(query, k_s[rows, :]), -1e30)
                top = jnp.max(near, axis=1, keepdims=True)
                if i:
                    past = against(query, k_s[:before_rows, :])
                    top = jnp.maximum(top, jnp.max(past, axis=1, keepdims=True))
                near = jnp.exp((near - top) * scale)
                total = jnp.sum(near, axis=1, keepdims=True)
                if i:
                    past = jnp.exp((past - top) * scale)
                    total = total + jnp.sum(past, axis=1, keepdims=True)
                share = 1.0 / total
                mixed = jnp.dot((near * share).astype(jnp.bfloat16), v_s[rows, :], preferred_element_type=jnp.float32)
                if i:
                    mixed = mixed + jnp.dot(
                        (past * share).astype(jnp.bfloat16), v_s[:before_rows, :], preferred_element_type=jnp.float32
                    )
                ctx[i, :, cols] = mixed.astype(jnp.bfloat16)
            return carry

        lax.fori_loop(0, HEADS_DEV, head, 0)

        if first:
            @pl.when(lead_near)
            def _():
                far_copy.wait_recv()
                add_rows(e_sum, QUARTER, e_far)
                for row_block in range(2):
                    src, dst = entry_copy(row_block, tensor)

                    @pl.when(is_owner(row_block))
                    def _(src=src, dst=dst):
                        pltpu.make_async_copy(src, dst, all_recv.at[tensor]).start()

                    @pl.when(jnp.logical_not(is_owner(row_block)))
                    def _(src=src, dst=dst, row_block=row_block):
                        remote(src, dst, all_send.at[row_block], all_recv.at[tensor], owner(row_block)).start()

        for copy in sends:
            copy.wait_send()
        if first:
            for copy in shares:
                copy.wait_send()

        def sib_copy(n):
            return remote(sib_out.at[n], sib_in.at[n], sib_send.at[l, n], sib_recv.at[l, n], sibling)

        def ring_copy(n, index):
            slot, rows, into, lane, device = ring_plan[index]
            dst = relay.at[n, lane] if into == "relay" else arrived.at[n, lane, rows]
            return remote(
                ring_out.at[n, slot, rows], dst, ring_send.at[l, n, index], ring_recv.at[l, n, index], device
            )

        def combine(n, slot, ring_slot, first_row, count, relayed):
            held = lax.rem(n, HELD)

            def rows_step(step, carry):
                rows = aligned(first_row + step * 16, 16)
                total = own_part[held, slot, rows, :] + sib_in[n, slot, rows, :].astype(jnp.float32)
                if relayed is not None:
                    total = total + relay[n, relayed, aligned(step * 16, 16), :].astype(jnp.float32)
                ring_out[n, ring_slot, rows, :] = total.astype(jnp.bfloat16)
                return carry

            lax.fori_loop(0, count // 16, rows_step, 0)

        def project_part(n):
            if first:
                handed(*wo_trade(n))
            held = lax.rem(n, HELD)

            def slot_step(slot, carry):
                chip = lax.rem(y + 6 - slot, RING)
                res = jnp.dot(ctx[chip], w_out[:, out_cols(n)], preferred_element_type=jnp.float32)
                top, bottom = res[:ROWS], res[ROWS:]
                own_part[held, slot] = jnp.where(core == 0, top, bottom)
                sib_out[n, slot] = jnp.where(core == 0, bottom, top).astype(jnp.bfloat16)
                return carry

            lax.fori_loop(0, 4, slot_step, 0)
            sib_copy(n).start()

        def send_part(n):
            sib_copy(n).wait_recv()
            combine(n, 0, 0, 0, ROWS, None)
            ring_copy(n, 0).start()
            ring_copy(n, 1).start()
            combine(n, 1, 1, HALF, HALF, None)
            ring_copy(n, 2).start()
            combine(n, 3, 2, 0, HALF, None)
            ring_copy(n, 3).start()

        def relay_part(n):
            ring_copy(n, 0).wait_recv()
            combine(n, 1, 1, 0, HALF, 0)
            ring_copy(n, 4).start()
            ring_copy(n, 1).wait_recv()
            combine(n, 3, 2, HALF, HALF, 1)
            ring_copy(n, 5).start()

        def finish_part(n):
            for index in (2, 3, 4, 5):
                ring_copy(n, index).wait_recv()
            held = lax.rem(n, HELD)

            def rows_step(step, carry):
                rows = aligned(step * 16, 16)
                total = own_part[held, 2, rows, :] + sib_in[n, 2, rows, :].astype(jnp.float32)
                total = total + arrived[n, 0, rows, :].astype(jnp.float32)
                total = total + arrived[n, 1, rows, :].astype(jnp.float32)
                total = x_s[l, rows, out_cols(n)].astype(jnp.float32) + total
                out_s[l, n, rows, :] = total
                if first:
                    next_s[n, rows, :] = total.astype(jnp.bfloat16)
                return carry

            lax.fori_loop(0, ROWS // 16, rows_step, 0)
            if first:
                @pl.when(has_next)
                def _():
                    next_copy(n).start()
            else:
                hand_over(*returned(1, n))

        def pipeline(i, carry):
            @pl.when((i >= 1) & (i < PARTS + 1))
            def _():
                send_part(i - 1)

            @pl.when(i < PARTS)
            def _():
                project_part(i)

            @pl.when((i >= 2) & (i < PARTS + 2))
            def _():
                relay_part(i - 2)

            @pl.when(i >= 3)
            def _():
                finish_part(i - 3)

            return carry

        lax.fori_loop(0, PARTS + 3, pipeline, 0)

        def sent(n, carry):
            sib_copy(n).wait_send()
            for index in range(6):
                ring_copy(n, index).wait_send()
            if first:
                handed_over(*wo_trade(n))

                @pl.when(has_next)
                def _():
                    next_copy(n).wait_send()

                @pl.when(has_prev)
                def _():
                    next_copy(n).wait_recv()

            return carry

        lax.fori_loop(0, PARTS, sent, 0)

    def returned(l, n):
        out = (first_out, second_out)[l]
        return (out_s.at[l, n], out.at[:, out_cols(n)], out_send.at[l, n], out_recv.at[l, n])

    lax.fori_loop(0, CHUNKS // 2, look_up, 0)
    handed(*gain_trade)
    handed(*x_trade)
    layer(0)

    @pl.when(enters)
    def _():
        for t in range(8):
            src, dst = entry_copy(0, t)
            remote(src, dst, all_send.at[0], all_recv.at[t], sibling).wait_recv()

    layer(1)

    for trade in (gain_trade, x_trade, *kv_trade, wq_trade):
        handed_over(*trade)

    @pl.when(core == 1)
    def _():
        core_copy.wait_send()

    @pl.when(lead)
    def _():
        for distance in (1, 2, 3):
            side_copy(distance).wait_send()

    @pl.when(lead_far)
    def _():
        far_copy.wait_send()

    @pl.when(lead_near)
    def _():
        for row_block in range(2):
            src, dst = entry_copy(row_block, tensor)

            @pl.when(jnp.logical_not(is_owner(row_block)))
            def _(src=src, dst=dst, row_block=row_block):
                remote(src, dst, all_send.at[row_block], all_recv.at[tensor], owner(row_block)).wait_send()

    def back(n, carry):
        for l in range(2):
            handed(*returned(l, n))
            handed_over(*returned(l, n))
        return carry

    lax.fori_loop(0, PARTS, back, 0)


def relay_layers(ids, *operands):
    bf16, f32 = jnp.bfloat16, jnp.float32
    dma = pltpu.SemaphoreType.DMA
    hbm = pl.BlockSpec(memory_space=pl.ANY)
    block = jax.ShapeDtypeStruct((ROWS, WIDTH), f32)
    return pl.pallas_call(
        relay_kernel,
        out_shape=(block, block),
        in_specs=[pl.BlockSpec(memory_space=pltpu.VMEM)] + [hbm] * len(operands),
        out_specs=(hbm, hbm),
        scratch_shapes=[
            pltpu.VMEM((2, ROWS, WIDTH), bf16),
            pltpu.VMEM((1, WIDTH), f32),
            pltpu.VMEM((WIDTH, 512), bf16),
            pltpu.VMEM((256, WIDTH), bf16),
            pltpu.VMEM((512, WIDTH), bf16),
            pltpu.VMEM((RING, PAIR, WIDTH), bf16),
            pltpu.VMEM((HEADS_DEV, TOKENS, HEAD_DIM), bf16),
            pltpu.VMEM((TOKENS, HEAD_DIM), bf16),
            pltpu.VMEM((TOKENS, HEAD_DIM), bf16),
            pltpu.VMEM((RING, PAIR, 512), bf16),
            pltpu.VMEM((HELD, 4, ROWS, PART), f32),
            pltpu.VMEM((PARTS, 4, ROWS, PART), bf16),
            pltpu.VMEM((PARTS, 4, ROWS, PART), bf16),
            pltpu.VMEM((PARTS, 3, ROWS, PART), bf16),
            pltpu.VMEM((PARTS, 2, HALF, PART), bf16),
            pltpu.VMEM((PARTS, 2, ROWS, PART), bf16),
            pltpu.VMEM((2, PARTS, ROWS, PART), f32),
            pltpu.VMEM((PARTS, ROWS, PART), bf16),
            pltpu.VMEM((2, CHUNK, COLS), bf16),
            pltpu.VMEM((TOKENS, COLS), bf16),
            pltpu.VMEM((TOKENS, COLS), bf16),
            pltpu.VMEM((3, QUARTER, COLS), bf16),
            pltpu.VMEM((QUARTER, COLS), bf16),
            pltpu.VMEM((QUARTER, COLS), bf16),
            dma((2,)), dma((4,)), dma((2, 14)), dma((2, RING, 2, 2)),
            dma((2, PARTS)), dma((2, PARTS)), dma((2, PARTS, 6)), dma((2, PARTS, 6)),
            dma((5 + PARTS,)), dma((5 + PARTS,)), dma((2, PARTS)), dma((2, PARTS)),
            dma((PARTS,)), dma((PARTS,)),
            dma((2,)), dma((3,)), dma((3,)), dma((2,)), dma((2,)), dma((8,)),
        ],
        compiler_params=pltpu.CompilerParams(
            collective_id=0, has_side_effects=True, vmem_limit_bytes=60 << 20
        ),
        cost_estimate=pl.CostEstimate(flops=32 * 10**9, bytes_accessed=32 << 20, transcendentals=8 << 20),
        name="relay_layers",
    )(ids, *operands)


def body(
    entry_symbol_ids,
    lookup_table_matrix,
    pending_batches,
    scale_factors,
    query_projector,
    key_projector,
    value_projector,
    result_projector,
):
    return relay_layers(
        entry_symbol_ids.reshape(TOKENS, 1), lookup_table_matrix, pending_batches, scale_factors,
        query_projector[0], key_projector[0].T, value_projector[0].T, result_projector[0],
    )


def solution(mesh):
    in_specs = (
        P(),
        P("pipe", "tensor"),
        P(("pipe", "tensor"), None),
        P("pipe", None),
        P("pipe", None, "tensor"),
        P("pipe", None, "tensor"),
        P("pipe", None, "tensor"),
        P("pipe", "tensor", None),
    )
    out_specs = (P(("pipe", "tensor"), None), P(("pipe", "tensor"), None))
    return jax.shard_map(body, mesh=mesh, in_specs=in_specs, out_specs=out_specs, check_vma=False)
```

time: 1340 us -> 265 us (0.20)
  the two profiles are of different devices: /device:TPU:1 before, /device:TPU:75 now
where the time goes in v5:
time: 265 us
  Pallas kernels  258 us (97%)
  local copies, waits for them, and re-layouts  6.29 us (2%)
    pallas_call x1, Pallas kernels, relay_layers(): pl.pallas_call(relay_kernel, out_shape=(block, block), in_specs=[pl.Block...  258 us

profile of v5, /device:TPU:75, one launch (start us, length us, event | category | flops | bytes accessed | tf_op | source)
XLA Modules:
  0.0 265.0 jit_solution(12188626142887005855)
XLA Ops:
  0.6 1.7 copy.10.ids_ref
  2.3 258.0 %relay_layers.1 = (f32[128,4096]{1,0:T(8,128)}, f32[128,4096]{1,0:T(8,128)}) custom-call(s32[1024,1]{1,0:T(8,128)} %copy.10.ids_ref, bf16[8192,512]{1,0:T(8,128)(2,1)} %table_hbm.1, bf16[128,4096]{1,0:T(8,128)(2,1)} %x_hbm.1, f32[1,4096]{1,0:T(1,128)} %gain_hbm.1, bf16[4096,512]{1,0:T(8,128)(2,1)} %bitcast.10, bf16[64,4096]{1,0:T(8,128)(2,1)} %bitcast.12, ...), custom_call_target="tpu_custom_call" | custom-call | flops 32000000000 | bytes 33554432 | tf_op jit(solution)/shard_map/relay_layers/pallas_call | solution.py:589
  260.4 0.0 copy-start
  260.4 3.3 %copy.13 = f32[128,4096]{1,0:T(8,128)} copy(f32[128,4096]{1,0:T(8,128)} %get-tuple-element.4) | data formatting | bytes 4194304
  263.7 0.0 copy-done
  263.7 1.3 copy.14
Async XLA Ops:
  260.4 3.3 %copy-start = (f32[128,4096]{1,0:T(8,128)S(1)}, f32[128,4096]{1,0:T(8,128)}, u32[]{:S(2)}) copy-start(f32[128,4096]{1,0:T(8,128)} %get-tuple-element.5) | copy-start | bytes 6291460
